TPU v7x, 32 devices: a whole 2x2x4 slice. The times are simulated.
32 devices in a mesh: win: 2 (over y), wide: 4 (over x, core), narrow: 4 (over z).
Axes of the slice: x: 2, y: 2, z: 4, core: 2. Of those that a mesh axis runs over, the one named last changes fastest.
Arguments:
- spectra: bfloat16 [64, 2, 128, 4096], P('win', None, 'wide', 'narrow'), parts along dimension 0, may hold values from -6 to 6
- live: int32 [256], P(('win', 'wide')), parts along dimension 0, may hold values 0 or 1
Outputs:
- correlation: float32 [512, 128, 128], P(('win', 'narrow'), 'wide'), parts along dimension 0
There are 2 independent parts, one for each index of `win`. A program takes and returns all parts, laid end to end along the dimension named above; each array names one. Nothing has to cross between parts.
All inputs are finite; a program needn't handle non-finite values. No bound on the sum of `live` on one device may be relied on, other than what follows from the above.
Results may differ from a plain program's by a relative error of at most 0.0085.
Values may be sent and summed in bfloat16 or wider, within the bound.
A program may use at most 256 MiB of HBM per device.

v0:
```python
import math

import jax
import jax.numpy as jnp
from jax import lax
from jax.sharding import PartitionSpec as P

F = 4096
L = 256
K = 4
S = 32


def from_behind(array, axis, by):
    length = lax.axis_size(axis)
    pairs = [(i, i + by) for i in range(length) if 0 <= i + by < length]
    return lax.ppermute(array, axis, pairs)


def per_device(spectra, live):
    block_size = spectra.shape[2]
    bins_here = spectra.shape[3]
    wide_pos = lax.axis_index("wide")
    narrow_pos = lax.axis_index("narrow")
    high = lax.Precision.HIGHEST
    spectra_list = [spectra]
    live_list = [live]
    for offset_step in range(1, K):
        received = from_behind((spectra, live), "wide", -offset_step)
        spectra_list.append(received[0])
        live_list.append(received[1])
    partners = jnp.concatenate(spectra_list, axis=2)
    partner_live = jnp.concatenate(live_list, axis=0)
    band_size = partners.shape[2]
    real_sum = jnp.einsum("scif,scjf->ijf", spectra, partners, preferred_element_type=jnp.float32)
    imag_sum = jnp.einsum(
        "sif,sjf->ijf", spectra[:, 0], partners[:, 1], preferred_element_type=jnp.float32
    ) - jnp.einsum(
        "sif,sjf->ijf", spectra[:, 1], partners[:, 0], preferred_element_type=jnp.float32
    )
    row_ids = wide_pos * block_size + jnp.arange(block_size, dtype=jnp.int32)
    partner_ids = wide_pos * block_size + jnp.arange(band_size, dtype=jnp.int32)
    keep_mask = (
        (row_ids[:, None] != partner_ids[None, :])
        & (live[:, None] > 0)
        & (partner_live[None, :] > 0)
    ).astype(jnp.float32)
    stack_scale = keep_mask[:, :, None] / jnp.float32(math.sqrt(S))
    cross_real = (real_sum * stack_scale).astype(jnp.bfloat16)
    cross_imag = (imag_sum * stack_scale).astype(jnp.bfloat16)
    lag_shift = jnp.arange(L, dtype=jnp.int32) - L // 2
    bin_index = narrow_pos * bins_here + jnp.arange(bins_here, dtype=jnp.int32)
    phase_angle = jnp.mod(bin_index[:, None] * lag_shift[None, :], F).astype(
        jnp.float32
    ) * jnp.float32(2.0 * math.pi / F)
    cos_table = jnp.cos(phase_angle)
    sin_table = jnp.sin(phase_angle)
    summed = jnp.einsum(
        "ijf,ft->tij", cross_real, cos_table, precision=high, preferred_element_type=jnp.float32
    ) - jnp.einsum(
        "ijf,ft->tij", cross_imag, sin_table, precision=high, preferred_element_type=jnp.float32
    )
    return lax.psum_scatter(
        (summed / jnp.float32(math.sqrt(F))).astype(jnp.bfloat16),
        "narrow",
        scatter_dimension=0,
        tiled=True,
    ).astype(jnp.float32)


def solution(mesh):
    placed = (P("win", None, "wide", "narrow"), P(("win", "wide")))
    return jax.shard_map(
        per_device,
        mesh=mesh,
        in_specs=placed,
        out_specs=P(("win", "narrow"), "wide", None),
        check_vma=False,
    )
```

profile of v0, /device:TPU:0, one launch (start us, length us, event | category | flops | bytes accessed | tf_op | source)
XLA Modules:
  0.0 467.4 jit_solution(15287607364935444645)
XLA Ops:
  6.5 0.0 reduce-scatter.2.cloned.1.call-start
  6.5 1.3 collective-permute-start
  7.8 1.3 collective-permute-start.1
  9.1 1.3 collective-permute-start.2
  10.4 1.3 collective-permute-start.5
  11.7 1.3 collective-permute-start.4
  13.0 23.2 %copy.5 = bf16[32,2,32,1024]{2,0,1,3:T(8,128)(2,1)} copy(bf16[32,2,32,1024]{3,2,1,0:T(8,128)(2,1)} %param.2) | data formatting | bytes 8388608 | tf_op args[0]
  36.2 0.0 copy-start.1
  36.2 0.0 copy-start
  36.3 5.1 %constant_dynamic-update-slice_fusion.3 = bf16[32,2,128,1024]{3,2,1,0:T(8,128)(2,1)} fusion(bf16[32,2,32,1024]{3,2,1,0:T(8,128)(2,1)} %param.2), kind=kLoop, calls=%fused_computation.29 | loop fusion | bytes 8388608
  41.4 0.0 copy-done.1
  41.4 0.0 copy-done
  41.4 1.8 slice_bitcast_fusion.2
  43.2 12.5 %copy.8 = bf16[32,32,1024]{1,0,2:T(8,128)(2,1)} copy(bf16[32,32,1024]{2,1,0:T(8,128)(2,1)} %get-tuple-element.8) | data formatting | bytes 4194304 | tf_op jit(solution)/shard_map/squeeze | solution.py:37
  55.7 137.3 %collective-permute-done.5 = s32[32]{0:T(128)S(1)} collective-permute-done((s32[32]{0:T(128)}, s32[32]{0:T(128)S(1)}, u32[]{:S(2)}, u32[]{:S(2)}) %collective-permute-start.5) | collective-permute-done | bytes 160 | tf_op jit(solution)/shard_map/ppermute | solution.py:17
  193.0 1.5 collective-permute-start.3
  194.5 12.1 %copy.11 = bf16[32,32,1024]{1,0,2:T(8,128)(2,1)} copy(bf16[32,32,1024]{2,1,0:T(8,128)(2,1)S(1)} %get-tuple-element.7) | data formatting | bytes 4194304 | tf_op jit(solution)/shard_map/squeeze | solution.py:39
  206.6 0.0 collective-permute-done.4
  206.6 0.0 collective-permute-done.3
  206.6 0.1 add_compare_fusion
  206.7 0.1 and_select_fusion
  206.7 0.0 collective-permute-done
  206.8 5.0 %constant_dynamic-update-slice_fusion.2 = bf16[32,2,128,1024]{3,2,1,0:T(8,128)(2,1)} fusion(bf16[32,2,128,1024]{3,2,1,0:T(8,128)(2,1)} %constant_dynamic-update-slice_fusion.3, bf16[32,2,32,1024]{3,2,1,0:T(8,128)(2,1)} %collective-permute-done), kind=kLoop, calls=%fused_computation.28 | loop fusion | bytes 8388608
  211.7 0.0 collective-permute-done.1
  211.7 5.0 %constant_dynamic-update-slice_fusion.1 = bf16[32,2,128,1024]{3,2,1,0:T(8,128)(2,1)} fusion(bf16[32,2,128,1024]{3,2,1,0:T(8,128)(2,1)} %constant_dynamic-update-slice_fusion.2, bf16[32,2,32,1024]{3,2,1,0:T(8,128)(2,1)} %collective-permute-done.1), kind=kLoop, calls=%fused_computation.27 | loop fusion | bytes 8388608
  216.7 0.0 collective-permute-done.2
  216.7 5.0 %constant_dynamic-update-slice_fusion = bf16[32,2,128,1024]{3,2,1,0:T(8,128)(2,1)} fusion(bf16[32,2,128,1024]{3,2,1,0:T(8,128)(2,1)} %constant_dynamic-update-slice_fusion.1, bf16[32,2,32,1024]{3,2,1,0:T(8,128)(2,1)} %collective-permute-done.2), kind=kLoop, calls=%fused_computation.26 | loop fusion | bytes 8388608 | tf_op jit(solution)/shard_map/concatenate | solution.py:32
  221.7 11.9 %slice_bitcast_fusion = (bf16[32,128,1024]{2,1,0:T(8,128)(2,1)}, bf16[32,128,1024]{2,1,0:T(8,128)(2,1)}) fusion(bf16[32,2,128,1024]{3,2,1,0:T(8,128)(2,1)} %constant_dynamic-update-slice_fusion), kind=kLoop, calls=%fused_computation.6 | loop fusion | bytes 33554432 | tf_op jit(solution)/shard_map/squeeze | solution.py:39
  233.6 23.9 %copy.4 = bf16[32,2,128,1024]{2,0,1,3:T(8,128)(2,1)} copy(bf16[32,2,128,1024]{3,2,1,0:T(8,128)(2,1)} %constant_dynamic-update-slice_fusion) | data formatting | bytes 33554432 | tf_op jit(solution)/shard_map/concatenate | solution.py:32
  257.6 12.5 %copy.7 = bf16[32,128,1024]{1,0,2:T(8,128)(2,1)} copy(bf16[32,128,1024]{2,1,0:T(8,128)(2,1)} %get-tuple-element.6) | data formatting | bytes 16777216 | tf_op jit(solution)/shard_map/squeeze | solution.py:37
  270.0 10.7 %fusion.28 = f32[1024,128,32]{1,2,0:T(8,128)} fusion(bf16[32,128,1024]{1,0,2:T(8,128)(2,1)} %copy.7, bf16[32,32,1024]{1,0,2:T(8,128)(2,1)} %copy.8), kind=kOutput, calls=%fused_computation.45 | convolution fusion | flops 268435456 | bytes 27262976 | tf_op jit(solution)/shard_map/sif,sjf->ijf/dot_general | solution.py:36
  280.8 16.5 %copy.9 = f32[1024,128,32]{0,1,2:T(8,128)} copy(f32[1024,128,32]{1,2,0:T(8,128)} %fusion.28) | data formatting | bytes 33554432 | tf_op jit(solution)/shard_map/sif,sjf->ijf/dot_general | solution.py:36
  297.3 12.5 %copy.10 = bf16[32,128,1024]{1,0,2:T(8,128)(2,1)} copy(bf16[32,128,1024]{2,1,0:T(8,128)(2,1)} %get-tuple-element.5) | data formatting | bytes 16777216 | tf_op jit(solution)/shard_map/squeeze | solution.py:39
  309.8 10.8 %fusion.29 = f32[1024,128,32]{1,2,0:T(8,128)} fusion(bf16[32,128,1024]{1,0,2:T(8,128)(2,1)} %copy.10, bf16[32,32,1024]{1,0,2:T(8,128)(2,1)} %copy.11), kind=kOutput, calls=%fused_computation.46 | convolution fusion | flops 268435456 | bytes 27262976 | tf_op jit(solution)/shard_map/sif,sjf->ijf/dot_general | solution.py:38
  320.6 16.6 %copy.12 = f32[1024,128,32]{0,1,2:T(8,128)} copy(f32[1024,128,32]{1,2,0:T(8,128)} %fusion.29) | data formatting | bytes 33554432 | tf_op jit(solution)/shard_map/sif,sjf->ijf/dot_general | solution.py:38
  337.2 18.8 %fusion.27 = f32[1024,128,32,1]{1,2,3,0:T(8,128)} fusion(bf16[32,2,128,1024]{2,0,1,3:T(8,128)(2,1)} %copy.4, bf16[32,2,32,1024]{2,0,1,3:T(8,128)(2,1)} %copy.5), kind=kOutput, calls=%fused_computation.44 | convolution fusion | flops 536870912 | bytes 37748736 | tf_op jit(solution)/shard_map/scif,scjf->ijf/dot_general | solution.py:35
  356.0 16.7 %copy.6 = f32[1024,128,32,1]{0,1,2,3:T(8,128)} copy(f32[1024,128,32,1]{1,2,3,0:T(8,128)} %fusion.27) | data formatting | bytes 33554432 | tf_op jit(solution)/shard_map/scif,scjf->ijf/dot_general | solution.py:35
  372.7 21.7 %fusion.2 = f32[256,32,128]{2,0,1:T(8,128)S(1)} fusion(f32[1024,128,32]{0,1,2:T(8,128)} %copy.9, f32[1024,128,32]{0,1,2:T(8,128)} %copy.12, f32[32,128]{1,0:T(8,128)S(1)} %and_select_fusion, s32[256]{0:T(256)S(1)} %iota_add_fusion.1, s32[1024]{0:T(1024)S(1)} %iota_add_fusion), kind=kOutput, calls=%fused_computation.4 | convolution fusion | flops 12901154816 | bytes 37770240 | tf_op jit(solution)/shard_map/ijf,ft->tij/dot_general | solution.py:60
  394.4 18.2 %multiply_convert_fusion = bf16[256,32,128]{2,0,1:T(8,128)(2,1)} fusion(f32[256,32,128]{2,0,1:T(8,128)S(1)} %fusion.2, f32[1024,128,32,1]{0,1,2,3:T(8,128)} %copy.6, f32[32,128]{1,0:T(8,128)S(1)} %and_select_fusion, s32[256]{0:T(256)S(1)} %iota_add_fusion.1, s32[1024]{0:T(1024)S(1)} %iota_add_fusion), kind=kOutput, calls=%fused_computation.10 | convolution fusion | flops 12900106240 | bytes 23090176 | tf_op jit(solution)/shard_map/ijf,ft->tij/dot_general | solution.py:58
  412.6 0.0 reduce-scatter.2.cloned.1.call-update
  412.6 45.1 %reduce-scatter.2.cloned.1.call-done = bf16[64,32,128]{2,0,1:T(8,128)(2,1)} async-done(((bf16[256,32,128]{2,0,1:T(8,128)(2,1)}), bf16[64,32,128]{2,0,1:T(8,128)(2,1)}) %reduce-scatter.2.cloned.1.call-update) | async-done | bytes 524304 | tf_op jit(solution)/shard_map/reduce_scatter | solution.py:63
  457.8 2.3 copy.3
  (5 shorter events, 0.0 us)
Async XLA Ops:
  6.5 451.2 %reduce-scatter.2.cloned.1.call-start = ((), (), s32[]{:S(2)}) async-start(), calls=%async_computation.1 | async-start | bytes 2621440 | tf_op jit(solution)/shard_map/reduce_scatter | solution.py:63
  6.5 200.2 %collective-permute-start = (bf16[32,2,32,1024]{3,2,1,0:T(8,128)(2,1)}, bf16[32,2,32,1024]{3,2,1,0:T(8,128)(2,1)}, u32[]{:S(2)}, u32[]{:S(2)}) collective-permute-start(bf16[32,2,32,1024]{3,2,1,0:T(8,128)(2,1)} %param.2), channel_id=1, source_target_pairs={{4,0},{8,4},{12,8},{5,1},{9,5},{13,9},{6,2},{10,6},{14,10},{7,3},{... | collective-permute-start | bytes 12582920 | tf_op jit(solution)/shard_map/ppermute | solution.py:17
  7.8 203.9 %collective-permute-start.1 = (bf16[32,2,32,1024]{3,2,1,0:T(8,128)(2,1)}, bf16[32,2,32,1024]{3,2,1,0:T(8,128)(2,1)}, u32[]{:S(2)}, u32[]{:S(2)}) collective-permute-start(bf16[32,2,32,1024]{3,2,1,0:T(8,128)(2,1)} %param.2), channel_id=1, source_target_pairs={{8,0},{12,4},{9,1},{13,5},{10,2},{14,6},{11,3},{15,7},{24,16},{28,... | collective-permute-start | bytes 12582920 | tf_op jit(solution)/shard_map/ppermute | solution.py:17
  9.1 207.6 %collective-permute-start.2 = (bf16[32,2,32,1024]{3,2,1,0:T(8,128)(2,1)}, bf16[32,2,32,1024]{3,2,1,0:T(8,128)(2,1)}, u32[]{:S(2)}, u32[]{:S(2)}) collective-permute-start(bf16[32,2,32,1024]{3,2,1,0:T(8,128)(2,1)} %param.2), channel_id=1, source_target_pairs={{12,0},{13,1},{14,2},{15,3},{28,16},{29,17},{30,18},{31,19}} | collective-permute-start | bytes 12582920 | tf_op jit(solution)/shard_map/ppermute | solution.py:17
  10.4 182.6 %collective-permute-start.5 = (s32[32]{0:T(128)}, s32[32]{0:T(128)S(1)}, u32[]{:S(2)}, u32[]{:S(2)}) collective-permute-start(s32[32]{0:T(128)} %param.3), channel_id=1, source_target_pairs={{12,0},{13,1},{14,2},{15,3},{28,16},{29,17},{30,18},{31,19}} | collective-permute-start | bytes 392 | tf_op jit(solution)/shard_map/ppermute | solution.py:17
  11.7 194.9 %collective-permute-start.4 = (s32[32]{0:T(128)}, s32[32]{0:T(128)S(1)}, u32[]{:S(2)}, u32[]{:S(2)}) collective-permute-start(s32[32]{0:T(128)} %param.3), channel_id=1, source_target_pairs={{8,0},{12,4},{9,1},{13,5},{10,2},{14,6},{11,3},{15,7},{24,16},{28,... | collective-permute-start | bytes 392 | tf_op jit(solution)/shard_map/ppermute | solution.py:17
  36.2 5.2 %copy-start.1 = (s32[32]{0:T(128)S(1)}, s32[32]{0:T(128)}, u32[]{:S(2)}) copy-start(s32[32]{0:T(128)} %param.3) | copy-start | bytes 388
  36.2 5.2 %copy-start = (bf16[32,2,32,1024]{3,2,1,0:T(8,128)(2,1)S(1)}, bf16[32,2,32,1024]{3,2,1,0:T(8,128)(2,1)}, u32[]{:S(2)}) copy-start(bf16[32,2,32,1024]{3,2,1,0:T(8,128)(2,1)} %param.2) | copy-start | bytes 12582916
  193.0 13.6 %collective-permute-start.3 = (s32[32]{0:T(128)S(1)}, s32[32]{0:T(128)S(1)}, u32[]{:S(2)}, u32[]{:S(2)}) collective-permute-start(s32[32]{0:T(128)S(1)} %copy-done.1), channel_id=1, source_target_pairs={{4,0},{8,4},{12,8},{5,1},{9,5},{13,9},{6,2},{10,6},{14,10},{7,3},{... | collective-permute-start | bytes 392 | tf_op jit(solution)/shard_map/ppermute | solution.py:17
Sparse Core Ops, SparseCore 0:
  412.8 44.9 reduce-scatter.1
where the time goes:
time: 473 us; the launch traced here: 467 us
  local copies, waits for them, and re-layouts  183 us (39%)
  waiting for transfers between devices  182 us (38%)
  matrix products  80.2 us (17%)
  between operations  13.9 us (3%)
  starting transfers between devices  7.9 us (2%)
    ppermute x6, waiting for transfers between devices, from_behind(): return lax.ppermute(array, axis, pairs)  137 us
    reduce_scatter x1, waiting for transfers between devices, per_device(): lax.psum_scatter((summed / jnp.float32(math.sqrt(F))).astype(jnp.bfloat16...  45.1 us
    unnamed x8, local copies, waits for them, and re-layouts  38.3 us
    concatenate x2, local copies, waits for them, and re-layouts, per_device(): partners = jnp.concatenate(spectra_list, axis=2)  28.9 us
    squeeze x2, local copies, waits for them, and re-layouts, per_device(): partners[:, 0]  24.4 us
    dot_general x1, matrix products, per_device(): jnp.einsum('ijf,ft->tij', cross_imag, sin_table, precision=high, preferre...  21.7 us
    dot_general x1, matrix products, per_device(): jnp.einsum('scif,scjf->ijf', spectra, partners, preferred_element_type=jn...  18.8 us
    dot_general x1, matrix products, per_device(): jnp.einsum('ijf,ft->tij', cross_real, cos_table, precision=high, preferre...  18.2 us
  transfers between devices with their start and end apart: 7, of which 2 were waited for; matrix products, arithmetic and copies ran while one was open for 14% of the time, Pallas kernels for 0%

commit v1 on v0

--- a/solution.py
+++ b/solution.py
@@ -1,14 +1,18 @@
+import functools
 import math
 
 import jax
 import jax.numpy as jnp
 from jax import lax
+from jax.experimental import pallas as pl
+from jax.experimental.pallas import tpu as pltpu
 from jax.sharding import PartitionSpec as P
 
 F = 4096
 L = 256
 K = 4
 S = 32
+BINS = 128
 
 
 def from_behind(array, axis, by):
@@ -17,7 +21,7 @@
     return lax.ppermute(array, axis, pairs)
 
 
-def per_device(spectra, live):
+def any_width(spectra, live):
     block_size = spectra.shape[2]
     bins_here = spectra.shape[3]
     wide_pos = lax.axis_index("wide")
@@ -68,10 +72,150 @@
     ).astype(jnp.float32)
 
 
+def correlate_kernel(crossing, meta_ref, *refs):
+    if crossing:
+        own, near, far_a, far_b, table, before, out, acc, spread, gram = refs
+        sources = (own, near, far_a, far_b)
+    else:
+        own, near, table, out, spread, gram = refs
+        acc = out
+        sources = (own, near)
+    step = pl.program_id(0)
+    points = 32 * len(sources)
+
+    @pl.when(step == 0)
+    def _():
+        if crossing:
+            acc[...] = before[...]
+        else:
+            acc[...] = jnp.zeros_like(acc)
+            spread[...] = jnp.zeros_like(spread)
+
+    def turn(s, carry):
+        for c in range(2):
+            tile = jnp.concatenate([ref[s, c] for ref in sources], axis=0)
+            turned = tile.astype(jnp.float32).T
+            spread[pl.ds(pl.multiple_of((c * S + s) * BINS, BINS), BINS), 0:points] = turned
+        return carry
+
+    lax.fori_loop(0, S, turn, 0, unroll=4)
+
+    def one_bin(f, carry):
+        both = spread[pl.ds(f, 2 * S, stride=BINS), :]
+        a, b = both[:S], both[S:]
+        plain = both.astype(jnp.bfloat16)
+        crossed = jnp.concatenate([b, -a], axis=0).astype(jnp.bfloat16)
+        right = jnp.concatenate([plain, crossed], axis=1)
+        product = lax.dot_general(
+            plain[:, :32], right, (((0,), (0,)), ((), ())), preferred_element_type=jnp.float32
+        )
+        gram[pl.ds(pl.multiple_of(f * 32, 32), 32), :] = product[:, :128]
+        gram[pl.ds(pl.multiple_of((BINS + f) * 32, 32), 32), :] = product[:, 128:]
+        return carry
+
+    lax.fori_loop(0, BINS, one_bin, 0, unroll=8)
+
+    lane = lax.broadcasted_iota(jnp.int32, (1, 128), 1)
+    sign = jnp.where((lane >= 64) & (meta_ref[1] == 1), -1.0, 1.0).astype(jnp.float32)
+
+    def two_rows(ip, carry):
+        real = [gram[pl.ds(2 * ip + r, BINS, stride=32), :] for r in range(2)]
+        imag = [gram[pl.ds(BINS * 32 + 2 * ip + r, BINS, stride=32), :] * sign for r in range(2)]
+        top = jnp.concatenate(real, axis=1)
+        low = jnp.concatenate(imag, axis=1)
+        right = jnp.concatenate([top, low], axis=0).astype(jnp.bfloat16)
+        cols = pl.ds(pl.multiple_of(ip * 256, 256), 256)
+        acc[:, cols] += jnp.dot(table[0], right, preferred_element_type=jnp.float32)
+        return carry
+
+    lax.fori_loop(0, 16, two_rows, 0, unroll=2)
+
+    if crossing:
+        @pl.when(step == pl.num_programs(0) - 1)
+        def _():
+            out[...] = (acc[...] * (1.0 / math.sqrt(S * F))).astype(out.dtype)
+
+
+def correlate(meta, own, near, far, table, before):
+    crossing = far is not None
+    half = own.shape[3] // BINS // 2
+    block = (S, 2, 32, BINS)
+    placed = pl.BlockSpec(block, lambda k, m: (0, 0, 0, m[0] + k))
+    near_by = pl.BlockSpec(block, lambda k, m: (0, 0, 0, k))
+    table_spec = pl.BlockSpec((1, L, 2 * BINS), lambda k, m: (m[0] + k, 0, 0))
+    whole = pl.BlockSpec((L, 4096), lambda k, m: (0, 0))
+    scratch = [pltpu.VMEM((2 * S * BINS, 128), jnp.float32), pltpu.VMEM((2 * BINS * 32, 128), jnp.float32)]
+    if crossing:
+        in_specs = [placed, placed, near_by, near_by, table_spec, whole]
+        operands = (own, near, far[0], far[1], table, before)
+        scratch = [pltpu.VMEM((L, 4096), jnp.float32)] + scratch
+    else:
+        in_specs = [placed, placed, table_spec]
+        operands = (own, near, table)
+    return pl.pallas_call(
+        functools.partial(correlate_kernel, crossing),
+        out_shape=jax.ShapeDtypeStruct((L, 4096), jnp.bfloat16 if crossing else jnp.float32),
+        grid_spec=pltpu.PrefetchScalarGridSpec(
+            num_scalar_prefetch=1, grid=(half,), in_specs=in_specs, out_specs=whole, scratch_shapes=scratch
+        ),
+        compiler_params=pltpu.CompilerParams(vmem_limit_bytes=48 * 2**20),
+        cost_estimate=pl.CostEstimate(flops=2 * 10**10, bytes_accessed=2**23, transcendentals=0),
+    )(meta, *operands)
+
+
+def two_chips(spectra, live):
+    bins_here = spectra.shape[3]
+    half = bins_here // 2
+    wide_pos = lax.axis_index("wide")
+    narrow_pos = lax.axis_index("narrow")
+    x, core = wide_pos // 2, wide_pos % 2
+    over_x = [(0, 2), (1, 3), (2, 0), (3, 1)]
+    on_chip = [(0, 1), (1, 0), (2, 3), (3, 2)]
+    leaving = lax.dynamic_slice_in_dim(spectra, (1 - x) * half, half, 3)
+    far_a = lax.ppermute(leaving, "wide", over_x)
+    near = lax.ppermute(spectra, "wide", on_chip)
+    far_b = lax.ppermute(far_a, "wide", on_chip)
+    all_live = lax.all_gather(live, "wide", tiled=True)
+
+    lag_shift = jnp.arange(L, dtype=jnp.int32) - L // 2
+    bin_index = narrow_pos * bins_here + jnp.arange(bins_here, dtype=jnp.int32)
+    bin_index = bin_index.reshape(-1, 1, BINS)
+    angle = jnp.mod(bin_index * lag_shift[None, :, None], F).astype(jnp.float32) * jnp.float32(
+        2.0 * math.pi / F
+    )
+    table = jnp.concatenate([jnp.cos(angle), -jnp.sin(angle)], axis=2).astype(jnp.bfloat16)
+
+    chunks = half // BINS
+    first = jnp.stack([(1 - x) * chunks, x]).astype(jnp.int32)
+    second = jnp.stack([x * chunks, x]).astype(jnp.int32)
+    before = correlate(first, spectra, near, None, table, None)
+    partial = correlate(second, spectra, near, (far_a, far_b), table, before)
+    mine = lax.psum_scatter(partial, "narrow", scatter_dimension=0, tiled=True)
+    mine = mine.reshape(-1, 32, 128)
+    back_a = lax.ppermute(mine[:, :, 64:96], "wide", [(2, 0), (3, 1)])
+    back_b = lax.ppermute(mine[:, :, 96:], "wide", [(2, 1), (3, 0)])
+    mine = mine.astype(jnp.float32)
+    far_1 = mine[:, :, 64:96] + jnp.swapaxes(back_a, 1, 2).astype(jnp.float32)
+    far_2 = mine[:, :, 96:] + jnp.swapaxes(back_b, 1, 2).astype(jnp.float32)
+    q1 = jnp.where(core == 0, mine[:, :, 32:64], far_2)
+    stacked = jnp.concatenate([mine[:, :, :32], q1, far_1, far_2], axis=2)
+    row = wide_pos * 32 + jnp.arange(32, dtype=jnp.int32)
+    partner = wide_pos * 32 + jnp.arange(128, dtype=jnp.int32)
+    partner_live = lax.dynamic_slice_in_dim(jnp.pad(all_live, (0, 128)), wide_pos * 32, 128)
+    keep = (
+        (row[:, None] != partner[None, :])
+        & (live[:, None] > 0)
+        & (partner_live[None, :] > 0)
+        & (partner[None, :] < 128)
+    )
+    return jnp.where(keep[None], stacked, 0.0)
+
+
 def solution(mesh):
     placed = (P("win", None, "wide", "narrow"), P(("win", "wide")))
+    fits = mesh.shape["wide"] == 4 and mesh.shape["narrow"] == 4
     return jax.shard_map(
-        per_device,
+        two_chips if fits else any_width,
         mesh=mesh,
         in_specs=placed,
         out_specs=P(("win", "narrow"), "wide", None),

time: 473 us -> 239 us (0.51); the launches traced: 467 us -> 239 us
  local copies, waits for them, and re-layouts: 183 us -> 10.7 us
  Pallas kernels: 0 us -> 90.9 us
  matrix products: 80.2 us -> 0 us
  waiting for transfers between devices: 182 us -> 103 us
  other arithmetic: 0.18 us -> 9.01 us
  blocking collectives: 0 us -> 5.2 us
    pallas_call x0 -> x2, Pallas kernels: none -> 90.9 us  [correlate(): pl.pallas_call(functools.partial(correlate_kernel, crossing), out_shape=j...]
    dot_general x5 -> x0, matrix products: 80.2 us -> none  [the longest x1 21.7 us: per_device(): jnp.einsum('ijf,ft->tij', cross_imag, sin_table, precision=high, preferre...]
    ppermute x6 -> x5, waiting for transfers between devices: 137 us -> 64.8 us  [the longest x1 42 us: two_chips(): far_a = lax.ppermute(leaving, 'wide', over_x)]
    squeeze x6 -> x0, local copies, waits for them, and re-layouts: 63.3 us -> none  [the longest x2 24.4 us: per_device(): partners[:, 0]]
    dot_general x3 -> x0, local copies, waits for them, and re-layouts: 49.8 us -> none  [the longest x1 16.7 us: per_device(): jnp.einsum('scif,scjf->ijf', spectra, partners, preferred_element_type=jn...]
    unnamed x8 -> x13, local copies, waits for them, and re-layouts: 38.3 us -> 6.89 us
    concatenate x2 -> x0, local copies, waits for them, and re-layouts: 28.9 us -> none  [per_device(): partners = jnp.concatenate(spectra_list, axis=2)]
    reduce_scatter x1, waiting for transfers between devices: 45.1 us -> 38.2 us  [two_chips(): mine = lax.psum_scatter(partial, 'narrow', scatter_dimension=0, tiled=True)]
  transfers between devices with their start and end apart: 7 -> 6, of which waited for: 2 -> 4; matrix products, arithmetic and copies ran while one was open for 14% -> 4% of each run, Pallas kernels for 0% -> 18%
where the time goes in v1:
time: 239 us
  waiting for transfers between devices  103 us (43%)
  Pallas kernels  90.9 us (38%)
  between operations  14.2 us (6%)
  local copies, waits for them, and re-layouts  10.7 us (4%)
  other arithmetic  9.01 us (4%)
  starting transfers between devices  5.52 us (2%)
  blocking collectives  5.2 us (2%)
    pallas_call x2, Pallas kernels, correlate(): pl.pallas_call(functools.partial(correlate_kernel, crossing), out_shape=j...  90.9 us
    ppermute x1, waiting for transfers between devices, two_chips(): far_a = lax.ppermute(leaving, 'wide', over_x)  42 us
    reduce_scatter x1, waiting for transfers between devices, two_chips(): mine = lax.psum_scatter(partial, 'narrow', scatter_dimension=0, tiled=True)  38.2 us
    ppermute x1, waiting for transfers between devices, two_chips(): back_b = lax.ppermute(mine[:, :, 96:], 'wide', [(2, 1), (3, 0)])  12.3 us
    ppermute x1, waiting for transfers between devices, two_chips(): back_a = lax.ppermute(mine[:, :, 64:96], 'wide', [(2, 0), (3, 1)])  10.5 us
    unnamed x13, local copies, waits for them, and re-layouts  6.89 us
    unnamed x1, blocking collectives  5.2 us
  transfers between devices with their start and end apart: 6, of which 4 were waited for; matrix products, arithmetic and copies ran while one was open for 4% of the time, Pallas kernels for 18%

profile of v1, /device:TPU:0, one launch (start us, length us, event | category | flops | bytes accessed | tf_op | source)
XLA Modules:
  0.0 238.6 jit_solution(17707992845419578710)
XLA Ops:
  6.5 0.0 reduce-scatter.2.cloned.1.call-start
  6.5 0.5 collective-permute-start
  7.0 3.2 %constant_dynamic-slice_fusion = bf16[32,2,32,512]{3,2,1,0:T(8,128)(2,1)} fusion(bf16[32,2,32,1024]{3,2,1,0:T(8,128)(2,1)} %refs_0_.3, s32[]{:T(128)S(6)} %select_n.37), kind=kLoop, calls=%fused_computation.27 | loop fusion | bytes 4194308 | tf_op jit(solution)/shard_map/dynamic_slice | solution.py:174
  10.2 2.5 %collective-permute-start.1 = (bf16[32,2,32,512]{3,2,1,0:T(8,128)(2,1)}, bf16[32,2,32,512]{3,2,1,0:T(8,128)(2,1)S(1)}, u32[]{:S(2)}, u32[]{:S(2)}) collective-permute-start(bf16[32,2,32,512]{3,2,1,0:T(8,128)(2,1)} %constant_dynamic-slice_fusion), channel_id=1, source_target_pairs={{0,8},{4,12},{8,0},{12,4},{1,9},{5,13},{9,1},{13,5},{2,10},{6,14},... | collective-permute-start | bytes 6291464 | tf_op jit(solution)/shard_map/ppermute | solution.py:175
  12.7 4.5 %cosine_convert_fusion = (bf16[8,256,128]{2,1,0:T(8,128)(2,1)S(1)}, bf16[8,256,128]{2,1,0:T(8,128)(2,1)S(1)}) fusion(s32[256]{0:T(256)S(1)} %iota_add_fusion, s32[8,128]{1,0:T(8,128)S(1)} %add_add_fusion), kind=kLoop, calls=%fused_computation.15 | loop fusion | flops 4456448 | bytes 1053696 | tf_op jit(solution)/shard_map/convert.2
  17.2 42.0 %collective-permute-done.1.refs_2_ = bf16[32,2,32,512]{3,2,1,0:T(8,128)(2,1)S(1)} collective-permute-done((bf16[32,2,32,512]{3,2,1,0:T(8,128)(2,1)}, bf16[32,2,32,512]{3,2,1,0:T(8,128)(2,1)S(1)}, u32[]{:S(2)}, u32[]{:S(2)}) %collective-permute-start.1) | collective-permute-done | bytes 2097184 | tf_op jit(solution)/shard_map/ppermute | solution.py:175
  59.2 0.0 collective-permute-start.2
  59.2 0.1 pad_add_fusion
  59.2 0.1 pad_maximum_fusion.refs_2_.refs_4_
  59.4 0.0 collective-permute-done.refs_1_
  59.4 43.8 %shard_map.28.refs_5_ = f32[256,4096]{1,0:T(8,128)S(1)} custom-call(s32[2]{0:T(128)S(1)} %get-tuple-element.16.meta_ref, bf16[32,2,32,1024]{3,2,1,0:T(8,128)(2,1)} %refs_0_.3, bf16[32,2,32,1024]{3,2,1,0:T(8,128)(2,1)} %collective-permute-done.refs_1_, bf16[8,256,256]{2,1,0:T(8,128)(2,1)S(1)} %pad_maximum_fusion.refs_2_.refs_4_), custom_call_target="tpu_custom_call" | custom-call | flops 20000000000 | bytes 8388608 | tf_op jit(solution)/shard_map/pallas_call | solution.py:155
  103.2 0.0 copy-start
  103.2 2.0 copy-done
  105.2 0.0 collective-permute-done.2.refs_3_
  105.2 0.0 copy-start.1
  105.2 1.3 copy-done.1
  106.5 47.1 %shard_map.29 = bf16[256,4096]{1,0:T(8,128)(2,1)} custom-call(s32[2]{0:T(128)S(1)} %get-tuple-element.15.meta_ref, bf16[32,2,32,1024]{3,2,1,0:T(8,128)(2,1)} %refs_0_.3, bf16[32,2,32,1024]{3,2,1,0:T(8,128)(2,1)} %collective-permute-done.refs_1_, bf16[32,2,32,512]{3,2,1,0:T(8,128)(2,1)S(1)} %collective-permute-done.1.refs_2_, ...), custom_call_target="tpu_custom_call" | custom-call | flops 20000000000 | bytes 8388608 | tf_op jit(solution)/shard_map/pallas_call | solution.py:155
  153.6 0.0 copy-start.3
  153.6 0.0 copy-start.2
  153.6 0.0 reduce-scatter.2.cloned.1.call-update
  153.6 0.6 copy-done.3
  154.3 0.6 dynamic-slice
  155.5 0.0 copy-done.2
  155.5 0.2 dynamic-update-slice
  155.8 5.2 %all-reduce.1 = s32[128]{0:T(128)S(1)} all-reduce(s32[128]{0:T(128)S(1)} %dynamic-update-slice), channel_id=1, replica_groups=mesh['win'=2,'wide'=4,'narrow'=4] {'wide'}, use_global_device_ids=true, to_apply=%add.1 | all-reduce | flops 128 | bytes 1024
  161.0 0.1 fusion.3
  161.1 0.1 and_and_fusion
  161.1 38.2 %reduce-scatter.2.cloned.1.call-done = bf16[64,4096]{1,0:T(8,128)(2,1)} async-done(((bf16[256,4096]{1,0:T(8,128)(2,1)}), bf16[64,4096]{1,0:T(8,128)(2,1)}) %reduce-scatter.2.cloned.1.call-update) | async-done | bytes 524304 | tf_op jit(solution)/shard_map/reduce_scatter | solution.py:193
  199.4 1.1 copy.6
  200.5 0.3 fusion.5
  200.9 1.3 collective-permute-start.3
  202.2 0.2 bitcast_convert_fusion
  202.3 1.0 copy.5
  203.3 1.3 collective-permute-start.4
  204.6 12.3 %collective-permute-done.3 = bf16[64,32,32]{2,1,0:T(8,128)(2,1)S(1)} collective-permute-done((bf16[64,32,32]{2,1,0:T(8,128)(2,1)S(1)}, bf16[64,32,32]{2,1,0:T(8,128)(2,1)S(1)}, u32[]{:S(2)}, u32[]{:S(2)}) %collective-permute-start.3) | collective-permute-done | bytes 131104 | tf_op jit(solution)/shard_map/ppermute | solution.py:196
  217.0 0.1 convert_bitcast_fusion
  217.1 0.3 copy.3
  217.4 10.5 %collective-permute-done.4 = bf16[64,32,32]{1,2,0:T(8,128)(2,1)} collective-permute-done((bf16[64,32,32]{1,2,0:T(8,128)(2,1)}, bf16[64,32,32]{1,2,0:T(8,128)(2,1)}, u32[]{:S(2)}, u32[]{:S(2)}) %collective-permute-start.4) | collective-permute-done | bytes 131104 | tf_op jit(solution)/shard_map/ppermute | solution.py:195
  228.0 2.0 fusion.4
  229.9 1.9 maximum_select_fusion
  (7 shorter events, 0.0 us)
Async XLA Ops:
  6.5 192.8 %reduce-scatter.2.cloned.1.call-start = ((), (), s32[]{:S(2)}) async-start(), calls=%async_computation.1 | async-start | bytes 2621440 | tf_op jit(solution)/shard_map/reduce_scatter | solution.py:193
  6.5 52.8 %collective-permute-start = (bf16[32,2,32,1024]{3,2,1,0:T(8,128)(2,1)}, bf16[32,2,32,1024]{3,2,1,0:T(8,128)(2,1)}, u32[]{:S(2)}, u32[]{:S(2)}) collective-permute-start(bf16[32,2,32,1024]{3,2,1,0:T(8,128)(2,1)} %refs_0_.3), channel_id=1, source_target_pairs={{0,4},{4,0},{8,12},{12,8},{1,5},{5,1},{9,13},{13,9},{2,6},{6,2},{1... | collective-permute-start | bytes 12582920 | tf_op jit(solution)/shard_map/ppermute | solution.py:176
  10.2 49.0 %collective-permute-start.1 = (bf16[32,2,32,512]{3,2,1,0:T(8,128)(2,1)}, bf16[32,2,32,512]{3,2,1,0:T(8,128)(2,1)S(1)}, u32[]{:S(2)}, u32[]{:S(2)}) collective-permute-start(bf16[32,2,32,512]{3,2,1,0:T(8,128)(2,1)} %constant_dynamic-slice_fusion), channel_id=1, source_target_pairs={{0,8},{4,12},{8,0},{12,4},{1,9},{5,13},{9,1},{13,5},{2,10},{6,14},... | collective-permute-start | bytes 6291464 | tf_op jit(solution)/shard_map/ppermute | solution.py:175
  59.2 46.0 %collective-permute-start.2 = (bf16[32,2,32,512]{3,2,1,0:T(8,128)(2,1)S(1)}, bf16[32,2,32,512]{3,2,1,0:T(8,128)(2,1)S(1)}, u32[]{:S(2)}, u32[]{:S(2)}) collective-permute-start(bf16[32,2,32,512]{3,2,1,0:T(8,128)(2,1)S(1)} %collective-permute-done.1.refs_2_), channel_id=1, source_target_pairs={{0,4},{4,0},{8,12},{12,8},{1,5},{5,1},{9,13},{13,9},{2,6},{6,2},{1... | collective-permute-start | bytes 6291464 | tf_op jit(solution)/shard_map/ppermute | solution.py:177
  103.2 2.0 copy-start
  105.2 1.3 copy-start.1
  153.6 0.7 copy-start.3
  153.6 1.9 copy-start.2
  200.9 16.1 %collective-permute-start.3 = (bf16[64,32,32]{2,1,0:T(8,128)(2,1)S(1)}, bf16[64,32,32]{2,1,0:T(8,128)(2,1)S(1)}, u32[]{:S(2)}, u32[]{:S(2)}) collective-permute-start(bf16[64,32,32]{2,1,0:T(8,128)(2,1)S(1)} %get-tuple-element.12), channel_id=1, source_target_pairs={{8,4},{12,0},{9,5},{13,1},{10,6},{14,2},{11,7},{15,3},{24,20},{28,... | collective-permute-start | bytes 393224 | tf_op jit(solution)/shard_map/ppermute | solution.py:196
  203.3 24.6 %collective-permute-start.4 = (bf16[64,32,32]{1,2,0:T(8,128)(2,1)}, bf16[64,32,32]{1,2,0:T(8,128)(2,1)}, u32[]{:S(2)}, u32[]{:S(2)}) collective-permute-start(bf16[64,32,32]{1,2,0:T(8,128)(2,1)} %copy.5), channel_id=1, source_target_pairs={{8,0},{12,4},{9,1},{13,5},{10,2},{14,6},{11,3},{15,7},{24,16},{28,... | collective-permute-start | bytes 393224 | tf_op jit(solution)/shard_map/ppermute | solution.py:195
Sparse Core Ops, SparseCore 0:
  153.8 45.5 reduce-scatter.1

commit v2 on v1

--- a/solution.py
+++ b/solution.py
@@ -146,11 +146,11 @@
     whole = pl.BlockSpec((L, 4096), lambda k, m: (0, 0))
     scratch = [pltpu.VMEM((2 * S * BINS, 128), jnp.float32), pltpu.VMEM((2 * BINS * 32, 128), jnp.float32)]
     if crossing:
-        in_specs = [placed, placed, near_by, near_by, table_spec, whole]
+        in_specs = [placed, near_by, near_by, near_by, table_spec, whole]
         operands = (own, near, far[0], far[1], table, before)
         scratch = [pltpu.VMEM((L, 4096), jnp.float32)] + scratch
     else:
-        in_specs = [placed, placed, table_spec]
+        in_specs = [placed, near_by, table_spec]
         operands = (own, near, table)
     return pl.pallas_call(
         functools.partial(correlate_kernel, crossing),
@@ -163,6 +163,14 @@
     )(meta, *operands)
 
 
+def fold(lags):
+    return jnp.concatenate(jnp.split(lags, 4, axis=0), axis=2)
+
+
+def unfold(folded):
+    return jnp.concatenate(jnp.split(folded, 4, axis=2), axis=0)
+
+
 def two_chips(spectra, live):
     bins_here = spectra.shape[3]
     half = bins_here // 2
@@ -172,10 +180,14 @@
     over_x = [(0, 2), (1, 3), (2, 0), (3, 1)]
     on_chip = [(0, 1), (1, 0), (2, 3), (3, 2)]
     leaving = lax.dynamic_slice_in_dim(spectra, (1 - x) * half, half, 3)
+    staying = lax.dynamic_slice_in_dim(spectra, x * half, half, 3)
     far_a = lax.ppermute(leaving, "wide", over_x)
-    near = lax.ppermute(spectra, "wide", on_chip)
+    near_first = lax.ppermute(leaving, "wide", on_chip)
+    near_second = lax.ppermute(staying, "wide", on_chip)
     far_b = lax.ppermute(far_a, "wide", on_chip)
-    all_live = lax.all_gather(live, "wide", tiled=True)
+    live_near = lax.ppermute(live, "wide", on_chip)
+    live_a = lax.ppermute(live, "wide", over_x)
+    live_b = lax.ppermute(live_a, "wide", on_chip)
 
     lag_shift = jnp.arange(L, dtype=jnp.int32) - L // 2
     bin_index = narrow_pos * bins_here + jnp.arange(bins_here, dtype=jnp.int32)
@@ -188,12 +200,12 @@
     chunks = half // BINS
     first = jnp.stack([(1 - x) * chunks, x]).astype(jnp.int32)
     second = jnp.stack([x * chunks, x]).astype(jnp.int32)
-    before = correlate(first, spectra, near, None, table, None)
-    partial = correlate(second, spectra, near, (far_a, far_b), table, before)
+    before = correlate(first, spectra, near_first, None, table, None)
+    partial = correlate(second, spectra, near_second, (far_a, far_b), table, before)
     mine = lax.psum_scatter(partial, "narrow", scatter_dimension=0, tiled=True)
     mine = mine.reshape(-1, 32, 128)
-    back_a = lax.ppermute(mine[:, :, 64:96], "wide", [(2, 0), (3, 1)])
-    back_b = lax.ppermute(mine[:, :, 96:], "wide", [(2, 1), (3, 0)])
+    back_a = unfold(lax.ppermute(fold(mine[:, :, 64:96]), "wide", [(2, 0), (3, 1)]))
+    back_b = unfold(lax.ppermute(fold(mine[:, :, 96:]), "wide", [(2, 1), (3, 0)]))
     mine = mine.astype(jnp.float32)
     far_1 = mine[:, :, 64:96] + jnp.swapaxes(back_a, 1, 2).astype(jnp.float32)
     far_2 = mine[:, :, 96:] + jnp.swapaxes(back_b, 1, 2).astype(jnp.float32)
@@ -201,7 +213,7 @@
     stacked = jnp.concatenate([mine[:, :, :32], q1, far_1, far_2], axis=2)
     row = wide_pos * 32 + jnp.arange(32, dtype=jnp.int32)
     partner = wide_pos * 32 + jnp.arange(128, dtype=jnp.int32)
-    partner_live = lax.dynamic_slice_in_dim(jnp.pad(all_live, (0, 128)), wide_pos * 32, 128)
+    partner_live = jnp.concatenate([live, jnp.where(core == 0, live_near, live_b), live_a, live_b])
     keep = (
         (row[:, None] != partner[None, :])
         & (live[:, None] > 0)

time: 239 us -> 234 us (0.979)
  waiting for transfers between devices: 103 us -> 88.5 us
  local copies, waits for them, and re-layouts: 10.7 us -> 16.7 us
  other arithmetic: 9.01 us -> 14.5 us
  blocking collectives: 5.2 us -> 0 us
  starting transfers between devices: 5.52 us -> 8.02 us
    ppermute x3 -> x7, waiting for transfers between devices: 22.9 us -> 7.29 us  [the longest x1 4.64 us: two_chips(): lax.ppermute(fold(mine[:, :, 64:96]), 'wide', [(2, 0), (3, 1)])]
    unnamed x1 -> x0, blocking collectives: 5.2 us -> none
    unnamed x13 -> x5, local copies, waits for them, and re-layouts: 6.89 us -> 3.15 us
    select_n x0 -> x2, other arithmetic: none -> 3.62 us  [the longest x1 3.62 us: two_chips(): q1 = jnp.where(core == 0, mine[:, :, 32:64], far_2)]
    select_n x0 -> x1, local copies, waits for them, and re-layouts: none -> 2.54 us  [two_chips(): q1 = jnp.where(core == 0, mine[:, :, 32:64], far_2)]
    ppermute x3 -> x7, starting transfers between devices: 3.02 us -> 5.08 us  [the longest x1 1.75 us: two_chips(): live_a = lax.ppermute(live, 'wide', over_x)]
  transfers between devices with their start and end apart: 6 -> 10, of which waited for: 4 -> 5; matrix products, arithmetic and copies ran while one was open for 4% -> 5% of each run, Pallas kernels for 18% -> 20%
where the time goes in v2:
time: 234 us
  Pallas kernels  92.8 us (40%)
  waiting for transfers between devices  88.5 us (38%)
  local copies, waits for them, and re-layouts  16.7 us (7%)
  other arithmetic  14.5 us (6%)
  between operations  13.5 us (6%)
  starting transfers between devices  8.02 us (3%)
    pallas_call x2, Pallas kernels, correlate(): pl.pallas_call(functools.partial(correlate_kernel, crossing), out_shape=j...  92.8 us
    ppermute x1, waiting for transfers between devices, two_chips(): far_a = lax.ppermute(leaving, 'wide', over_x)  40.9 us
    reduce_scatter x1, waiting for transfers between devices, two_chips(): mine = lax.psum_scatter(partial, 'narrow', scatter_dimension=0, tiled=True)  40.3 us
    dynamic_slice x1, local copies, waits for them, and re-layouts, two_chips(): leaving = lax.dynamic_slice_in_dim(spectra, (1 - x) * half, half, 3)  4.8 us
  transfers between devices with their start and end apart: 10, of which 5 were waited for; matrix products, arithmetic and copies ran while one was open for 5% of the time, Pallas kernels for 20%

profile of v2, /device:TPU:0, one launch (start us, length us, event | category | flops | bytes accessed | tf_op | source)
XLA Modules:
  0.0 234.0 jit_solution(10587172194515047435)
XLA Ops:
  6.5 0.0 reduce-scatter.2.cloned.1.call-start
  6.5 4.8 %constant_dynamic-slice_fusion = (bf16[32,2,32,512]{3,2,1,0:T(8,128)(2,1)}, bf16[32,2,32,512]{3,2,1,0:T(8,128)(2,1)}) fusion(bf16[32,2,32,1024]{3,2,1,0:T(8,128)(2,1)} %refs_0_.3, s32[]{:T(128)S(6)} %select_n.48, s32[]{:T(128)S(6)} %select_n.47), kind=kLoop, calls=%fused_computation.24 | loop fusion | bytes 8388616 | tf_op jit(solution)/shard_map/dynamic_slice | solution.py:182
  11.3 2.9 %collective-permute-start.4 = (bf16[32,2,32,512]{3,2,1,0:T(8,128)(2,1)}, bf16[32,2,32,512]{3,2,1,0:T(8,128)(2,1)}, u32[]{:S(2)}, u32[]{:S(2)}) collective-permute-start(bf16[32,2,32,512]{3,2,1,0:T(8,128)(2,1)} %get-tuple-element.8), channel_id=1, source_target_pairs={{0,8},{4,12},{8,0},{12,4},{1,9},{5,13},{9,1},{13,5},{2,10},{6,14},... | collective-permute-start | bytes 6291464 | tf_op jit(solution)/shard_map/ppermute | solution.py:184
  14.3 0.0 collective-permute-start.6
  14.3 0.5 collective-permute-start.3
  14.8 4.5 %cosine_convert_fusion = (bf16[8,256,128]{2,1,0:T(8,128)(2,1)S(1)}, bf16[8,256,128]{2,1,0:T(8,128)(2,1)S(1)}) fusion(s32[256]{0:T(256)S(1)} %iota_add_fusion, s32[8,128]{1,0:T(8,128)S(1)} %add_add_fusion), kind=kLoop, calls=%fused_computation.14 | loop fusion | flops 4456448 | bytes 1053696 | tf_op jit(solution)/shard_map/convert.2
  19.3 40.9 %collective-permute-done.4.refs_2_ = bf16[32,2,32,512]{3,2,1,0:T(8,128)(2,1)} collective-permute-done((bf16[32,2,32,512]{3,2,1,0:T(8,128)(2,1)}, bf16[32,2,32,512]{3,2,1,0:T(8,128)(2,1)}, u32[]{:S(2)}, u32[]{:S(2)}) %collective-permute-start.4) | collective-permute-done | bytes 2097184 | tf_op jit(solution)/shard_map/ppermute | solution.py:184
  60.2 0.0 collective-permute-start.5
  60.2 0.1 pad_add_fusion
  60.3 0.1 pad_maximum_fusion.refs_2_.refs_4_
  60.4 0.0 collective-permute-done.6.refs_1_
  60.4 45.8 %shard_map.28.refs_5_ = f32[256,4096]{1,0:T(8,128)} custom-call(s32[2]{0:T(128)S(1)} %get-tuple-element.29.meta_ref, bf16[32,2,32,1024]{3,2,1,0:T(8,128)(2,1)} %refs_0_.3, bf16[32,2,32,512]{3,2,1,0:T(8,128)(2,1)} %collective-permute-done.6.refs_1_, bf16[8,256,256]{2,1,0:T(8,128)(2,1)S(1)} %pad_maximum_fusion.refs_2_.refs_4_), custom_call_target="tpu_custom_call" | custom-call | flops 20000000000 | bytes 8388608 | tf_op jit(solution)/shard_map/pallas_call | solution.py:155
  106.2 0.0 collective-permute-done.3.refs_1_
  106.2 0.0 collective-permute-done.5.refs_3_
  106.2 0.0 copy-start.1
  106.2 1.4 copy-done.1
  107.6 47.0 %shard_map.29 = bf16[256,4096]{1,0:T(8,128)(2,1)} custom-call(s32[2]{0:T(128)S(1)} %get-tuple-element.28.meta_ref, bf16[32,2,32,1024]{3,2,1,0:T(8,128)(2,1)} %refs_0_.3, bf16[32,2,32,512]{3,2,1,0:T(8,128)(2,1)S(1)} %collective-permute-done.3.refs_1_, bf16[32,2,32,512]{3,2,1,0:T(8,128)(2,1)} %collective-permute-done.4.refs_2_, ...), custom_call_target="tpu_custom_call" | custom-call | flops 20000000000 | bytes 8388608 | tf_op jit(solution)/shard_map/pallas_call | solution.py:155
  154.6 0.0 copy-start
  154.6 0.0 reduce-scatter.2.cloned.1.call-update
  154.6 0.6 copy-done
  155.3 1.7 collective-permute-start.1
  157.0 0.2 collective-permute-start
  157.3 1.5 collective-permute-done.1
  158.8 0.0 collective-permute-start.2
  158.8 0.0 collective-permute-done
  158.8 1.1 collective-permute-done.2
  159.9 0.1 add_compare_fusion
  160.0 40.3 %reduce-scatter.2.cloned.1.call-done = bf16[64,4096]{1,0:T(8,128)(2,1)} async-done(((bf16[256,4096]{1,0:T(8,128)(2,1)}), bf16[64,4096]{1,0:T(8,128)(2,1)}) %reduce-scatter.2.cloned.1.call-update) | async-done | bytes 524304 | tf_op jit(solution)/shard_map/reduce_scatter | solution.py:205
  200.3 1.1 copy.15
  201.5 0.3 fusion.3
  201.8 0.2 pad_maximum_fusion.1
  202.0 1.3 collective-permute-start.7
  203.3 0.1 and_and_fusion
  203.4 1.0 copy.10
  204.4 2.5 %convert_element_type.20 = f32[64,32,128]{1,2,0:T(8,128)} convert(bf16[64,32,128]{1,2,0:T(8,128)(2,1)S(1)} %copy.10) | non-fusion elementwise | flops 262144 | bytes 1572864 | tf_op jit(solution)/shard_map/convert_element_type | solution.py:209
  206.9 1.1 slice.26
  208.0 0.2 pad_maximum_fusion.2
  208.2 1.3 collective-permute-start.8
  209.5 1.6 copy.11
  211.1 0.0 collective-permute-done.7
  211.1 0.2 fusion.5
  211.2 4.6 %collective-permute-done.8 = bf16[16,32,128]{2,1,0:T(8,128)(2,1)S(1)} collective-permute-done((bf16[16,32,128]{2,1,0:T(8,128)(2,1)S(1)}, bf16[16,32,128]{2,1,0:T(8,128)(2,1)S(1)}, u32[]{:S(2)}, u32[]{:S(2)}) %collective-permute-start.8) | collective-permute-done | bytes 131104 | tf_op jit(solution)/shard_map/ppermute | solution.py:207
  215.9 0.2 fusion.4
  216.1 3.6 %slice_select_fusion = (f32[64,32,32]{1,2,0:T(8,128)}, f32[64,32,32]{1,2,0:T(8,128)S(1)}, f32[64,32,32]{1,2,0:T(8,128)}) fusion(f32[64,32,128]{1,2,0:T(8,128)} %convert_element_type.20, pred[]{:T(512)S(6)} %eq.8, bf16[16,32,32]{2,1,0:T(8,128)(2,1)S(1)} %get-tuple-element.23, bf16[16,32,32]{2,1,0:T(8,128)(2,1)S(1)} %get-tuple-element.24, ...), kind=kLoop, calls=%fused_computation.10 | loop fusion | flops 720896 | bytes 1835009 | tf_op jit(solution)/shard_map/jit(_where)/select_n | solution.py:212
  219.7 0.3 copy.14
  220.0 1.6 copy.13
  221.6 2.5 %copy.12 = f32[64,32,32]{2,1,0:T(8,128)} copy(f32[64,32,32]{1,2,0:T(8,128)} %get-tuple-element.5) | data formatting | bytes 524288 | tf_op jit(solution)/shard_map/jit(_where)/select_n | solution.py:212
  224.1 3.1 %maximum_select_fusion = f32[64,32,128]{2,1,0:T(8,128)} fusion(f32[64,32,32]{2,1,0:T(8,128)S(1)} %copy.14, f32[64,32,32]{2,1,0:T(8,128)S(1)} %copy.13, f32[64,32,32]{2,1,0:T(8,128)} %copy.12, f32[64,32,32]{2,1,0:T(8,128)S(1)} %copy.11, pred[32,128]{1,0:T(8,128)(4,1)S(1)} %and_and_fusion), kind=kLoop, calls=%fused_computation.12 | loop fusion | flops 1048576 | bytes 2101248 | tf_op jit(solution)/shard_map/jit(_where)/select_n | solution.py:223
  (7 shorter events, 0.0 us)
Async XLA Ops:
  6.5 193.8 %reduce-scatter.2.cloned.1.call-start = ((), (), s32[]{:S(2)}) async-start(), calls=%async_computation.1 | async-start | bytes 2621440 | tf_op jit(solution)/shard_map/reduce_scatter | solution.py:205
  11.3 48.9 %collective-permute-start.4 = (bf16[32,2,32,512]{3,2,1,0:T(8,128)(2,1)}, bf16[32,2,32,512]{3,2,1,0:T(8,128)(2,1)}, u32[]{:S(2)}, u32[]{:S(2)}) collective-permute-start(bf16[32,2,32,512]{3,2,1,0:T(8,128)(2,1)} %get-tuple-element.8), channel_id=1, source_target_pairs={{0,8},{4,12},{8,0},{12,4},{1,9},{5,13},{9,1},{13,5},{2,10},{6,14},... | collective-permute-start | bytes 6291464 | tf_op jit(solution)/shard_map/ppermute | solution.py:184
  14.3 46.2 %collective-permute-start.6 = (bf16[32,2,32,512]{3,2,1,0:T(8,128)(2,1)}, bf16[32,2,32,512]{3,2,1,0:T(8,128)(2,1)}, u32[]{:S(2)}, u32[]{:S(2)}) collective-permute-start(bf16[32,2,32,512]{3,2,1,0:T(8,128)(2,1)} %get-tuple-element.8), channel_id=1, source_target_pairs={{0,4},{4,0},{8,12},{12,8},{1,5},{5,1},{9,13},{13,9},{2,6},{6,2},{1... | collective-permute-start | bytes 6291464 | tf_op jit(solution)/shard_map/ppermute | solution.py:185
  14.3 91.9 %collective-permute-start.3 = (bf16[32,2,32,512]{3,2,1,0:T(8,128)(2,1)}, bf16[32,2,32,512]{3,2,1,0:T(8,128)(2,1)S(1)}, u32[]{:S(2)}, u32[]{:S(2)}) collective-permute-start(bf16[32,2,32,512]{3,2,1,0:T(8,128)(2,1)} %get-tuple-element.9), channel_id=1, source_target_pairs={{0,4},{4,0},{8,12},{12,8},{1,5},{5,1},{9,13},{13,9},{2,6},{6,2},{1... | collective-permute-start | bytes 6291464 | tf_op jit(solution)/shard_map/ppermute | solution.py:186
  60.2 46.0 %collective-permute-start.5 = (bf16[32,2,32,512]{3,2,1,0:T(8,128)(2,1)}, bf16[32,2,32,512]{3,2,1,0:T(8,128)(2,1)S(1)}, u32[]{:S(2)}, u32[]{:S(2)}) collective-permute-start(bf16[32,2,32,512]{3,2,1,0:T(8,128)(2,1)} %collective-permute-done.4.refs_2_), channel_id=1, source_target_pairs={{0,4},{4,0},{8,12},{12,8},{1,5},{5,1},{9,13},{13,9},{2,6},{6,2},{1... | collective-permute-start | bytes 6291464 | tf_op jit(solution)/shard_map/ppermute | solution.py:187
  106.2 1.4 copy-start.1
  154.6 0.7 copy-start
  155.3 3.5 %collective-permute-start.1 = (s32[32]{0:T(128)S(1)}, s32[32]{0:T(128)S(1)}, u32[]{:S(2)}, u32[]{:S(2)}) collective-permute-start(s32[32]{0:T(128)S(1)} %copy-done), channel_id=1, source_target_pairs={{0,8},{4,12},{8,0},{12,4},{1,9},{5,13},{9,1},{13,5},{2,10},{6,14},... | collective-permute-start | bytes 392 | tf_op jit(solution)/shard_map/ppermute | solution.py:189
  157.0 1.8 collective-permute-start
  158.8 1.1 collective-permute-start.2
  202.0 9.0 %collective-permute-start.7 = (bf16[16,32,128]{2,1,0:T(8,128)(2,1)S(1)}, bf16[16,32,128]{2,1,0:T(8,128)(2,1)S(1)}, u32[]{:S(2)}, u32[]{:S(2)}) collective-permute-start(bf16[16,32,128]{2,1,0:T(8,128)(2,1)S(1)} %pad_maximum_fusion.1), channel_id=1, source_target_pairs={{8,4},{12,0},{9,5},{13,1},{10,6},{14,2},{11,7},{15,3},{24,20},{28,... | collective-permute-start | bytes 393224 | tf_op jit(solution)/shard_map/ppermute | solution.py:208
  208.2 7.7 %collective-permute-start.8 = (bf16[16,32,128]{2,1,0:T(8,128)(2,1)S(1)}, bf16[16,32,128]{2,1,0:T(8,128)(2,1)S(1)}, u32[]{:S(2)}, u32[]{:S(2)}) collective-permute-start(bf16[16,32,128]{2,1,0:T(8,128)(2,1)S(1)} %pad_maximum_fusion.2), channel_id=1, source_target_pairs={{8,0},{12,4},{9,1},{13,5},{10,2},{14,6},{11,3},{15,7},{24,16},{28,... | collective-permute-start | bytes 393224 | tf_op jit(solution)/shard_map/ppermute | solution.py:207
Sparse Core Ops, SparseCore 0:
  154.8 45.5 reduce-scatter.1

commit v3 on v2

--- a/solution.py
+++ b/solution.py
@@ -72,12 +72,15 @@
     ).astype(jnp.float32)
 
 
-def correlate_kernel(crossing, meta_ref, *refs):
+def correlate_kernel(crossing, starting, meta_ref, *refs):
     if crossing:
         own, near, far_a, far_b, table, before, out, acc, spread, gram = refs
         sources = (own, near, far_a, far_b)
     else:
-        own, near, table, out, spread, gram = refs
+        if starting:
+            own, near, table, out, spread, gram = refs
+        else:
+            own, near, table, before, out, spread, gram = refs
         acc = out
         sources = (own, near)
     step = pl.program_id(0)
@@ -85,10 +88,8 @@
 
     @pl.when(step == 0)
     def _():
-        if crossing:
-            acc[...] = before[...]
-        else:
-            acc[...] = jnp.zeros_like(acc)
+        acc[...] = jnp.zeros_like(acc) if starting else before[...]
+        if not crossing:
             spread[...] = jnp.zeros_like(spread)
 
     def turn(s, carry):
@@ -113,7 +114,7 @@
         gram[pl.ds(pl.multiple_of((BINS + f) * 32, 32), 32), :] = product[:, 128:]
         return carry
 
-    lax.fori_loop(0, BINS, one_bin, 0, unroll=8)
+    lax.fori_loop(0, BINS, one_bin, 0, unroll=32)
 
     lane = lax.broadcasted_iota(jnp.int32, (1, 128), 1)
     sign = jnp.where((lane >= 64) & (meta_ref[1] == 1), -1.0, 1.0).astype(jnp.float32)
@@ -128,7 +129,7 @@
         acc[:, cols] += jnp.dot(table[0], right, preferred_element_type=jnp.float32)
         return carry
 
-    lax.fori_loop(0, 16, two_rows, 0, unroll=2)
+    lax.fori_loop(0, 16, two_rows, 0, unroll=8)
 
     if crossing:
         @pl.when(step == pl.num_programs(0) - 1)
@@ -136,13 +137,12 @@
             out[...] = (acc[...] * (1.0 / math.sqrt(S * F))).astype(out.dtype)
 
 
-def correlate(meta, own, near, far, table, before):
+def correlate(meta, own, near, far, table, before, skip, chunks):
     crossing = far is not None
-    half = own.shape[3] // BINS // 2
     block = (S, 2, 32, BINS)
-    placed = pl.BlockSpec(block, lambda k, m: (0, 0, 0, m[0] + k))
-    near_by = pl.BlockSpec(block, lambda k, m: (0, 0, 0, k))
-    table_spec = pl.BlockSpec((1, L, 2 * BINS), lambda k, m: (m[0] + k, 0, 0))
+    placed = pl.BlockSpec(block, lambda k, m: (0, 0, 0, m[0] + skip + k))
+    near_by = pl.BlockSpec(block, lambda k, m: (0, 0, 0, skip + k))
+    table_spec = pl.BlockSpec((1, L, 2 * BINS), lambda k, m: (m[0] + skip + k, 0, 0))
     whole = pl.BlockSpec((L, 4096), lambda k, m: (0, 0))
     scratch = [pltpu.VMEM((2 * S * BINS, 128), jnp.float32), pltpu.VMEM((2 * BINS * 32, 128), jnp.float32)]
     if crossing:
@@ -152,14 +152,17 @@
     else:
         in_specs = [placed, near_by, table_spec]
         operands = (own, near, table)
+        if before is not None:
+            in_specs.append(whole)
+            operands += (before,)
     return pl.pallas_call(
-        functools.partial(correlate_kernel, crossing),
+        functools.partial(correlate_kernel, crossing, before is None),
         out_shape=jax.ShapeDtypeStruct((L, 4096), jnp.bfloat16 if crossing else jnp.float32),
         grid_spec=pltpu.PrefetchScalarGridSpec(
-            num_scalar_prefetch=1, grid=(half,), in_specs=in_specs, out_specs=whole, scratch_shapes=scratch
+            num_scalar_prefetch=1, grid=(chunks,), in_specs=in_specs, out_specs=whole, scratch_shapes=scratch
         ),
         compiler_params=pltpu.CompilerParams(vmem_limit_bytes=48 * 2**20),
-        cost_estimate=pl.CostEstimate(flops=2 * 10**10, bytes_accessed=2**23, transcendentals=0),
+        cost_estimate=pl.CostEstimate(flops=chunks * 5 * 10**9, bytes_accessed=2**23, transcendentals=0),
     )(meta, *operands)
 
 
@@ -184,7 +187,6 @@
     far_a = lax.ppermute(leaving, "wide", over_x)
     near_first = lax.ppermute(leaving, "wide", on_chip)
     near_second = lax.ppermute(staying, "wide", on_chip)
-    far_b = lax.ppermute(far_a, "wide", on_chip)
     live_near = lax.ppermute(live, "wide", on_chip)
     live_a = lax.ppermute(live, "wide", over_x)
     live_b = lax.ppermute(live_a, "wide", on_chip)
@@ -200,8 +202,11 @@
     chunks = half // BINS
     first = jnp.stack([(1 - x) * chunks, x]).astype(jnp.int32)
     second = jnp.stack([x * chunks, x]).astype(jnp.int32)
-    before = correlate(first, spectra, near_first, None, table, None)
-    partial = correlate(second, spectra, near_second, (far_a, far_b), table, before)
+    before = correlate(first, spectra, near_first, None, table, None, 0, chunks // 2)
+    far_a, before = lax.optimization_barrier((far_a, before))
+    far_b = lax.ppermute(far_a, "wide", on_chip)
+    before = correlate(first, spectra, near_first, None, table, before, chunks // 2, chunks - chunks // 2)
+    partial = correlate(second, spectra, near_second, (far_a, far_b), table, before, 0, chunks)
     mine = lax.psum_scatter(partial, "narrow", scatter_dimension=0, tiled=True)
     mine = mine.reshape(-1, 32, 128)
     back_a = unfold(lax.ppermute(fold(mine[:, :, 64:96]), "wide", [(2, 0), (3, 1)]))

time: 234 us -> 195 us (0.83)
  Pallas kernels: 92.8 us -> 72.8 us
  waiting for transfers between devices: 88.5 us -> 70.1 us
    pallas_call x2 -> x3, Pallas kernels: 92.8 us -> 72.8 us  [correlate(): pl.pallas_call(functools.partial(correlate_kernel, crossing, before is No...]
    ppermute x1, waiting for transfers between devices: 40.9 us -> 23 us  [two_chips(): far_a = lax.ppermute(leaving, 'wide', over_x)]
    ppermute x1, waiting for transfers between devices: 4.64 us -> 0.01 us  [two_chips(): lax.ppermute(fold(mine[:, :, 64:96]), 'wide', [(2, 0), (3, 1)])]
    ppermute x1, waiting for transfers between devices: 0.01 us -> 4.12 us  [two_chips(): lax.ppermute(fold(mine[:, :, 96:]), 'wide', [(2, 1), (3, 0)])]
  transfers between devices with their start and end apart: 10 -> 10, of which waited for: 5 -> 5; matrix products, arithmetic and copies ran while one was open for 5% -> 6% of each run, Pallas kernels for 20% -> 20%
where the time goes in v3:
time: 195 us; the launch traced here: 194 us
  Pallas kernels  72.8 us (37%)
  waiting for transfers between devices  70.1 us (36%)
  local copies, waits for them, and re-layouts  15.5 us (8%)
  other arithmetic  14.6 us (7%)
  between operations  13.5 us (7%)
  starting transfers between devices  7.92 us (4%)
    pallas_call x3, Pallas kernels, correlate(): pl.pallas_call(functools.partial(correlate_kernel, crossing, before is No...  72.8 us
    reduce_scatter x1, waiting for transfers between devices, two_chips(): mine = lax.psum_scatter(partial, 'narrow', scatter_dimension=0, tiled=True)  40.3 us
    ppermute x1, waiting for transfers between devices, two_chips(): far_a = lax.ppermute(leaving, 'wide', over_x)  23 us
    dynamic_slice x1, local copies, waits for them, and re-layouts, two_chips(): leaving = lax.dynamic_slice_in_dim(spectra, (1 - x) * half, half, 3)  4.91 us
    another operation x1, other arithmetic  4.52 us
    ppermute x1, waiting for transfers between devices, two_chips(): lax.ppermute(fold(mine[:, :, 96:]), 'wide', [(2, 1), (3, 0)])  4.12 us
  transfers between devices with their start and end apart: 10, of which 5 were waited for; matrix products, arithmetic and copies ran while one was open for 6% of the time, Pallas kernels for 20%

profile of v3, /device:TPU:0, one launch (start us, length us, event | category | flops | bytes accessed | tf_op | source)
XLA Modules:
  0.0 194.3 jit_solution(4349828966183938211)
XLA Ops:
  6.5 0.0 reduce-scatter.2.cloned.1.call-start
  6.5 4.9 %constant_dynamic-slice_fusion = (bf16[32,2,32,512]{3,2,1,0:T(8,128)(2,1)}, bf16[32,2,32,512]{3,2,1,0:T(8,128)(2,1)}) fusion(bf16[32,2,32,1024]{3,2,1,0:T(8,128)(2,1)} %refs_0_.5, s32[]{:T(128)S(6)} %select_n.48, s32[]{:T(128)S(6)} %select_n.47), kind=kLoop, calls=%fused_computation.24 | loop fusion | bytes 8388616 | tf_op jit(solution)/shard_map/dynamic_slice | solution.py:185
  11.4 0.5 collective-permute-start.5
  11.9 2.5 %collective-permute-start.4 = (bf16[32,2,32,512]{3,2,1,0:T(8,128)(2,1)}, bf16[32,2,32,512]{3,2,1,0:T(8,128)(2,1)}, u32[]{:S(2)}, u32[]{:S(2)}) collective-permute-start(bf16[32,2,32,512]{3,2,1,0:T(8,128)(2,1)} %get-tuple-element.12), channel_id=1, source_target_pairs={{0,8},{4,12},{8,0},{12,4},{1,9},{5,13},{9,1},{13,5},{2,10},{6,14},... | collective-permute-start | bytes 6291464 | tf_op jit(solution)/shard_map/ppermute | solution.py:187
  14.4 0.2 collective-permute-start.3
  14.6 0.1 pad_add_fusion.1.meta_ref
  14.7 4.5 %cosine_convert_fusion = (bf16[8,256,128]{2,1,0:T(8,128)(2,1)S(1)}, bf16[8,256,128]{2,1,0:T(8,128)(2,1)S(1)}) fusion(s32[256]{0:T(256)S(1)} %iota_add_fusion, s32[8,128]{1,0:T(8,128)S(1)} %add_add_fusion), kind=kLoop, calls=%fused_computation.14 | loop fusion | flops 4456448 | bytes 1053696 | tf_op jit(solution)/shard_map/convert.2
  19.2 0.1 pad_maximum_fusion.refs_2_.refs_4_
  19.4 0.0 collective-permute-done.5.refs_1_
  19.4 18.6 %shard_map.28.refs_3_ = f32[256,4096]{1,0:T(8,128)} custom-call(s32[2]{0:T(128)S(1)} %pad_add_fusion.1.meta_ref, bf16[32,2,32,1024]{3,2,1,0:T(8,128)(2,1)} %refs_0_.5, bf16[32,2,32,512]{3,2,1,0:T(8,128)(2,1)} %collective-permute-done.5.refs_1_, bf16[8,256,256]{2,1,0:T(8,128)(2,1)S(1)} %pad_maximum_fusion.refs_2_.refs_4_), custom_call_target="tpu_custom_call" | custom-call | flops 10000000000 | bytes 8388608 | tf_op jit(solution)/shard_map/pallas_call | solution.py:158
  38.0 23.0 %collective-permute-done.4.refs_2_ = bf16[32,2,32,512]{3,2,1,0:T(8,128)(2,1)} collective-permute-done((bf16[32,2,32,512]{3,2,1,0:T(8,128)(2,1)}, bf16[32,2,32,512]{3,2,1,0:T(8,128)(2,1)}, u32[]{:S(2)}, u32[]{:S(2)}) %collective-permute-start.4) | collective-permute-done | bytes 2097184 | tf_op jit(solution)/shard_map/ppermute | solution.py:187
  61.0 0.0 collective-permute-start.6
  61.0 0.1 pad_add_fusion.meta_ref
  61.1 20.0 %shard_map.29.refs_5_ = f32[256,4096]{1,0:T(8,128)} custom-call(s32[2]{0:T(128)S(1)} %pad_add_fusion.1.meta_ref, bf16[32,2,32,1024]{3,2,1,0:T(8,128)(2,1)} %refs_0_.5, bf16[32,2,32,512]{3,2,1,0:T(8,128)(2,1)} %collective-permute-done.5.refs_1_, bf16[8,256,256]{2,1,0:T(8,128)(2,1)S(1)} %pad_maximum_fusion.refs_2_.refs_4_, f32[256,4096]{1,0:T(8,128)} %shard_map.28.refs_3_), custom_call_target="tpu_custom_call" | custom-call | flops 10000000000 | bytes 8388608 | tf_op jit(solution)/shard_map/pallas_call | solution.py:158
  81.1 0.0 collective-permute-done.3.refs_1_
  81.1 0.0 collective-permute-done.6.refs_3_
  81.1 34.2 %shard_map.30 = bf16[256,4096]{1,0:T(8,128)(2,1)} custom-call(s32[2]{0:T(128)S(1)} %pad_add_fusion.meta_ref, bf16[32,2,32,1024]{3,2,1,0:T(8,128)(2,1)} %refs_0_.5, bf16[32,2,32,512]{3,2,1,0:T(8,128)(2,1)S(1)} %collective-permute-done.3.refs_1_, bf16[32,2,32,512]{3,2,1,0:T(8,128)(2,1)} %collective-permute-done.4.refs_2_, ...), custom_call_target="tpu_custom_call" | custom-call | flops 20000000000 | bytes 8388608 | tf_op jit(solution)/shard_map/pallas_call | solution.py:158
  115.2 0.0 copy-start
  115.2 0.0 reduce-scatter.2.cloned.1.call-update
  115.3 0.6 copy-done
  115.9 1.7 collective-permute-start.1
  117.6 0.2 collective-permute-start
  117.9 1.5 collective-permute-done.1
  119.4 0.0 collective-permute-start.2
  119.4 0.0 collective-permute-done
  119.4 1.1 collective-permute-done.2
  120.6 0.1 add_compare_fusion
  120.6 40.3 %reduce-scatter.2.cloned.1.call-done = bf16[64,4096]{1,0:T(8,128)(2,1)} async-done(((bf16[256,4096]{1,0:T(8,128)(2,1)}), bf16[64,4096]{1,0:T(8,128)(2,1)}) %reduce-scatter.2.cloned.1.call-update) | async-done | bytes 524304 | tf_op jit(solution)/shard_map/reduce_scatter | solution.py:210
  160.9 1.1 copy.15
  162.1 0.3 fusion.3
  162.4 0.2 pad_maximum_fusion.2
  162.6 1.5 collective-permute-start.8
  164.1 0.1 and_and_fusion
  164.2 1.0 copy.10
  165.2 2.5 %convert_element_type.20 = f32[64,32,128]{1,2,0:T(8,128)} convert(bf16[64,32,128]{1,2,0:T(8,128)(2,1)S(1)} %copy.10) | non-fusion elementwise | flops 262144 | bytes 1572864 | tf_op jit(solution)/shard_map/convert_element_type | solution.py:214
  167.7 1.1 slice.26
  168.8 0.2 pad_maximum_fusion.1
  169.0 1.3 collective-permute-start.7
  170.3 1.6 copy.11
  171.8 0.0 collective-permute-done.8
  171.9 0.2 fusion.4
  172.0 4.1 %collective-permute-done.7 = bf16[16,32,128]{2,1,0:T(8,128)(2,1)S(1)} collective-permute-done((bf16[16,32,128]{2,1,0:T(8,128)(2,1)S(1)}, bf16[16,32,128]{2,1,0:T(8,128)(2,1)S(1)}, u32[]{:S(2)}, u32[]{:S(2)}) %collective-permute-start.7) | collective-permute-done | bytes 131104 | tf_op jit(solution)/shard_map/ppermute | solution.py:213
  176.2 0.2 fusion.5
  176.3 3.6 %slice_select_fusion = (f32[64,32,32]{1,2,0:T(8,128)S(1)}, f32[64,32,32]{1,2,0:T(8,128)}, f32[64,32,32]{1,2,0:T(8,128)}) fusion(f32[64,32,128]{1,2,0:T(8,128)} %convert_element_type.20, pred[]{:T(512)S(6)} %eq.8, bf16[16,32,32]{2,1,0:T(8,128)(2,1)S(1)} %get-tuple-element.27, bf16[16,32,32]{2,1,0:T(8,128)(2,1)S(1)} %get-tuple-element.28, ...), kind=kLoop, calls=%fused_computation.10 | loop fusion | flops 720896 | bytes 1835009 | tf_op jit(solution)/shard_map/jit(_where)/select_n | solution.py:217
  180.0 0.3 copy.12
  180.3 1.6 copy.13
  181.9 2.5 %copy.14 = f32[64,32,32]{2,1,0:T(8,128)} copy(f32[64,32,32]{1,2,0:T(8,128)} %get-tuple-element.10) | data formatting | bytes 524288 | tf_op jit(solution)/shard_map/add | solution.py:216
  184.4 3.1 %maximum_select_fusion = f32[64,32,128]{2,1,0:T(8,128)} fusion(f32[64,32,32]{2,1,0:T(8,128)} %copy.14, f32[64,32,32]{2,1,0:T(8,128)S(1)} %copy.13, f32[64,32,32]{2,1,0:T(8,128)S(1)} %copy.12, f32[64,32,32]{2,1,0:T(8,128)S(1)} %copy.11, pred[32,128]{1,0:T(8,128)(4,1)S(1)} %and_and_fusion), kind=kLoop, calls=%fused_computation.12 | loop fusion | flops 1048576 | bytes 2101248 | tf_op jit(solution)/shard_map/jit(_where)/select_n | solution.py:228
  (7 shorter events, 0.0 us)
Async XLA Ops:
  6.5 154.4 %reduce-scatter.2.cloned.1.call-start = ((), (), s32[]{:S(2)}) async-start(), calls=%async_computation.1 | async-start | bytes 2621440 | tf_op jit(solution)/shard_map/reduce_scatter | solution.py:210
  11.4 7.9 %collective-permute-start.5 = (bf16[32,2,32,512]{3,2,1,0:T(8,128)(2,1)}, bf16[32,2,32,512]{3,2,1,0:T(8,128)(2,1)}, u32[]{:S(2)}, u32[]{:S(2)}) collective-permute-start(bf16[32,2,32,512]{3,2,1,0:T(8,128)(2,1)} %get-tuple-element.12), channel_id=1, source_target_pairs={{0,4},{4,0},{8,12},{12,8},{1,5},{5,1},{9,13},{13,9},{2,6},{6,2},{1... | collective-permute-start | bytes 6291464 | tf_op jit(solution)/shard_map/ppermute | solution.py:188
  11.9 49.1 %collective-permute-start.4 = (bf16[32,2,32,512]{3,2,1,0:T(8,128)(2,1)}, bf16[32,2,32,512]{3,2,1,0:T(8,128)(2,1)}, u32[]{:S(2)}, u32[]{:S(2)}) collective-permute-start(bf16[32,2,32,512]{3,2,1,0:T(8,128)(2,1)} %get-tuple-element.12), channel_id=1, source_target_pairs={{0,8},{4,12},{8,0},{12,4},{1,9},{5,13},{9,1},{13,5},{2,10},{6,14},... | collective-permute-start | bytes 6291464 | tf_op jit(solution)/shard_map/ppermute | solution.py:187
  14.4 66.7 %collective-permute-start.3 = (bf16[32,2,32,512]{3,2,1,0:T(8,128)(2,1)}, bf16[32,2,32,512]{3,2,1,0:T(8,128)(2,1)S(1)}, u32[]{:S(2)}, u32[]{:S(2)}) collective-permute-start(bf16[32,2,32,512]{3,2,1,0:T(8,128)(2,1)} %get-tuple-element.13), channel_id=1, source_target_pairs={{0,4},{4,0},{8,12},{12,8},{1,5},{5,1},{9,13},{13,9},{2,6},{6,2},{1... | collective-permute-start | bytes 6291464 | tf_op jit(solution)/shard_map/ppermute | solution.py:189
  61.0 20.1 %collective-permute-start.6 = (bf16[32,2,32,512]{3,2,1,0:T(8,128)(2,1)}, bf16[32,2,32,512]{3,2,1,0:T(8,128)(2,1)}, u32[]{:S(2)}, u32[]{:S(2)}) collective-permute-start(bf16[32,2,32,512]{3,2,1,0:T(8,128)(2,1)} %collective-permute-done.4.refs_2_), channel_id=1, source_target_pairs={{0,4},{4,0},{8,12},{12,8},{1,5},{5,1},{9,13},{13,9},{2,6},{6,2},{1... | collective-permute-start | bytes 6291464 | tf_op jit(solution)/shard_map/ppermute | solution.py:207
  115.2 0.7 copy-start
  115.9 3.5 %collective-permute-start.1 = (s32[32]{0:T(128)S(1)}, s32[32]{0:T(128)S(1)}, u32[]{:S(2)}, u32[]{:S(2)}) collective-permute-start(s32[32]{0:T(128)S(1)} %copy-done), channel_id=1, source_target_pairs={{0,8},{4,12},{8,0},{12,4},{1,9},{5,13},{9,1},{13,5},{2,10},{6,14},... | collective-permute-start | bytes 392 | tf_op jit(solution)/shard_map/ppermute | solution.py:191
  117.6 1.8 collective-permute-start
  119.4 1.1 collective-permute-start.2
  162.6 9.2 %collective-permute-start.8 = (bf16[16,32,128]{2,1,0:T(8,128)(2,1)S(1)}, bf16[16,32,128]{2,1,0:T(8,128)(2,1)S(1)}, u32[]{:S(2)}, u32[]{:S(2)}) collective-permute-start(bf16[16,32,128]{2,1,0:T(8,128)(2,1)S(1)} %pad_maximum_fusion.2), channel_id=1, source_target_pairs={{8,0},{12,4},{9,1},{13,5},{10,2},{14,6},{11,3},{15,7},{24,16},{28,... | collective-permute-start | bytes 393224 | tf_op jit(solution)/shard_map/ppermute | solution.py:212
  169.0 7.2 %collective-permute-start.7 = (bf16[16,32,128]{2,1,0:T(8,128)(2,1)S(1)}, bf16[16,32,128]{2,1,0:T(8,128)(2,1)S(1)}, u32[]{:S(2)}, u32[]{:S(2)}) collective-permute-start(bf16[16,32,128]{2,1,0:T(8,128)(2,1)S(1)} %pad_maximum_fusion.1), channel_id=1, source_target_pairs={{8,4},{12,0},{9,5},{13,1},{10,6},{14,2},{11,7},{15,3},{24,20},{28,... | collective-permute-start | bytes 393224 | tf_op jit(solution)/shard_map/ppermute | solution.py:213
Sparse Core Ops, SparseCore 0:
  115.4 45.4 reduce-scatter.1

commit v4 on v3

--- a/solution.py
+++ b/solution.py
@@ -95,11 +95,11 @@
     def turn(s, carry):
         for c in range(2):
             tile = jnp.concatenate([ref[s, c] for ref in sources], axis=0)
-            turned = tile.astype(jnp.float32).T
+            turned = tile.T.astype(jnp.float32)
             spread[pl.ds(pl.multiple_of((c * S + s) * BINS, BINS), BINS), 0:points] = turned
         return carry
 
-    lax.fori_loop(0, S, turn, 0, unroll=4)
+    lax.fori_loop(0, S, turn, 0, unroll=16)
 
     def one_bin(f, carry):
         both = spread[pl.ds(f, 2 * S, stride=BINS), :]
@@ -129,7 +129,7 @@
         acc[:, cols] += jnp.dot(table[0], right, preferred_element_type=jnp.float32)
         return carry
 
-    lax.fori_loop(0, 16, two_rows, 0, unroll=8)
+    lax.fori_loop(0, 16, two_rows, 0, unroll=16)
 
     if crossing:
         @pl.when(step == pl.num_programs(0) - 1)
@@ -202,10 +202,9 @@
     chunks = half // BINS
     first = jnp.stack([(1 - x) * chunks, x]).astype(jnp.int32)
     second = jnp.stack([x * chunks, x]).astype(jnp.int32)
-    before = correlate(first, spectra, near_first, None, table, None, 0, chunks // 2)
+    before = correlate(first, spectra, near_first, None, table, None, 0, chunks)
     far_a, before = lax.optimization_barrier((far_a, before))
     far_b = lax.ppermute(far_a, "wide", on_chip)
-    before = correlate(first, spectra, near_first, None, table, before, chunks // 2, chunks - chunks // 2)
     partial = correlate(second, spectra, near_second, (far_a, far_b), table, before, 0, chunks)
     mine = lax.psum_scatter(partial, "narrow", scatter_dimension=0, tiled=True)
     mine = mine.reshape(-1, 32, 128)

time: 195 us -> 177 us (0.908)
  Pallas kernels: 72.8 us -> 61.5 us
  waiting for transfers between devices: 70.1 us -> 63.5 us
    ppermute x1, waiting for transfers between devices: 23 us -> 11.4 us  [two_chips(): far_a = lax.ppermute(leaving, 'wide', over_x)]
    pallas_call x3 -> x2, Pallas kernels: 72.8 us -> 61.5 us  [correlate(): pl.pallas_call(functools.partial(correlate_kernel, crossing, before is No...]
    ppermute x1, waiting for transfers between devices: 0.01 us -> 4.64 us  [two_chips(): lax.ppermute(fold(mine[:, :, 64:96]), 'wide', [(2, 0), (3, 1)])]
    ppermute x1, waiting for transfers between devices: 0.01 us -> 4.42 us  [two_chips(): far_b = lax.ppermute(far_a, 'wide', on_chip)]
    ppermute x1, waiting for transfers between devices: 4.12 us -> 0.01 us  [two_chips(): lax.ppermute(fold(mine[:, :, 96:]), 'wide', [(2, 1), (3, 0)])]
    select_n x1, local copies, waits for them, and re-layouts: 0.33 us -> 2.54 us  [two_chips(): q1 = jnp.where(core == 0, mine[:, :, 32:64], far_2)]
    add x1, local copies, waits for them, and re-layouts: 2.54 us -> 0.33 us  [two_chips(): far_2 = mine[:, :, 96:] + jnp.swapaxes(back_b, 1, 2).astype(jnp.float32)]
  transfers between devices with their start and end apart: 10 -> 10, of which waited for: 5 -> 6; matrix products, arithmetic and copies ran while one was open for 6% -> 7% of each run, Pallas kernels for 20% -> 17%
where the time goes in v4:
time: 177 us; the launch traced here: 176 us
  waiting for transfers between devices  63.5 us (36%)
  Pallas kernels  61.5 us (35%)
  local copies, waits for them, and re-layouts  15.4 us (9%)
  other arithmetic  14.6 us (8%)
  between operations  13.5 us (8%)
  starting transfers between devices  7.68 us (4%)
    pallas_call x2, Pallas kernels, correlate(): pl.pallas_call(functools.partial(correlate_kernel, crossing, before is No...  61.5 us
    reduce_scatter x1, waiting for transfers between devices, two_chips(): mine = lax.psum_scatter(partial, 'narrow', scatter_dimension=0, tiled=True)  40.1 us
    ppermute x1, waiting for transfers between devices, two_chips(): far_a = lax.ppermute(leaving, 'wide', over_x)  11.4 us
    dynamic_slice x1, local copies, waits for them, and re-layouts, two_chips(): leaving = lax.dynamic_slice_in_dim(spectra, (1 - x) * half, half, 3)  4.89 us
    ppermute x1, waiting for transfers between devices, two_chips(): lax.ppermute(fold(mine[:, :, 64:96]), 'wide', [(2, 0), (3, 1)])  4.64 us
    another operation x1, other arithmetic  4.52 us
    ppermute x1, waiting for transfers between devices, two_chips(): far_b = lax.ppermute(far_a, 'wide', on_chip)  4.42 us
    select_n x1, other arithmetic, two_chips(): q1 = jnp.where(core == 0, mine[:, :, 32:64], far_2)  3.62 us
  transfers between devices with their start and end apart: 10, of which 6 were waited for; matrix products, arithmetic and copies ran while one was open for 7% of the time, Pallas kernels for 17%

profile of v4, /device:TPU:0, one launch (start us, length us, event | category | flops | bytes accessed | tf_op | source)
XLA Modules:
  0.0 176.2 jit_solution(14871235410201172607)
XLA Ops:
  6.5 0.0 reduce-scatter.2.cloned.1.call-start
  6.5 4.9 %constant_dynamic-slice_fusion = (bf16[32,2,32,512]{3,2,1,0:T(8,128)(2,1)}, bf16[32,2,32,512]{3,2,1,0:T(8,128)(2,1)}) fusion(bf16[32,2,32,1024]{3,2,1,0:T(8,128)(2,1)} %refs_0_.3, s32[]{:T(128)S(6)} %select_n.48, s32[]{:T(128)S(6)} %select_n.47), kind=kLoop, calls=%fused_computation.24 | loop fusion | bytes 8388616 | tf_op jit(solution)/shard_map/dynamic_slice | solution.py:185
  11.4 0.5 collective-permute-start.5
  11.9 2.5 %collective-permute-start.4 = (bf16[32,2,32,512]{3,2,1,0:T(8,128)(2,1)}, bf16[32,2,32,512]{3,2,1,0:T(8,128)(2,1)}, u32[]{:S(2)}, u32[]{:S(2)}) collective-permute-start(bf16[32,2,32,512]{3,2,1,0:T(8,128)(2,1)} %get-tuple-element.12), channel_id=1, source_target_pairs={{0,8},{4,12},{8,0},{12,4},{1,9},{5,13},{9,1},{13,5},{2,10},{6,14},... | collective-permute-start | bytes 6291464 | tf_op jit(solution)/shard_map/ppermute | solution.py:187
  14.4 0.2 collective-permute-start.3
  14.6 4.5 %cosine_convert_fusion = (bf16[8,256,128]{2,1,0:T(8,128)(2,1)S(1)}, bf16[8,256,128]{2,1,0:T(8,128)(2,1)S(1)}) fusion(s32[256]{0:T(256)S(1)} %iota_add_fusion, s32[8,128]{1,0:T(8,128)S(1)} %add_add_fusion), kind=kLoop, calls=%fused_computation.14 | loop fusion | flops 4456448 | bytes 1053696 | tf_op jit(solution)/shard_map/convert.2
  19.1 0.1 pad_add_fusion.1.meta_ref
  19.2 0.1 pad_maximum_fusion.refs_2_.refs_4_
  19.3 0.0 collective-permute-done.5.refs_1_
  19.4 30.3 %shard_map.28.refs_5_ = f32[256,4096]{1,0:T(8,128)} custom-call(s32[2]{0:T(128)S(1)} %pad_add_fusion.1.meta_ref, bf16[32,2,32,1024]{3,2,1,0:T(8,128)(2,1)} %refs_0_.3, bf16[32,2,32,512]{3,2,1,0:T(8,128)(2,1)} %collective-permute-done.5.refs_1_, bf16[8,256,256]{2,1,0:T(8,128)(2,1)S(1)} %pad_maximum_fusion.refs_2_.refs_4_), custom_call_target="tpu_custom_call" | custom-call | flops 20000000000 | bytes 8388608 | tf_op jit(solution)/shard_map/pallas_call | solution.py:158
  49.6 11.4 %collective-permute-done.4.refs_2_ = bf16[32,2,32,512]{3,2,1,0:T(8,128)(2,1)} collective-permute-done((bf16[32,2,32,512]{3,2,1,0:T(8,128)(2,1)}, bf16[32,2,32,512]{3,2,1,0:T(8,128)(2,1)}, u32[]{:S(2)}, u32[]{:S(2)}) %collective-permute-start.4) | collective-permute-done | bytes 2097184 | tf_op jit(solution)/shard_map/ppermute | solution.py:187
  61.0 0.0 collective-permute-start.6
  61.0 0.1 pad_add_fusion.meta_ref
  61.1 0.0 collective-permute-done.3.refs_1_
  61.1 4.4 %collective-permute-done.6.refs_3_ = bf16[32,2,32,512]{3,2,1,0:T(8,128)(2,1)} collective-permute-done((bf16[32,2,32,512]{3,2,1,0:T(8,128)(2,1)}, bf16[32,2,32,512]{3,2,1,0:T(8,128)(2,1)}, u32[]{:S(2)}, u32[]{:S(2)}) %collective-permute-start.6) | collective-permute-done | bytes 2097184 | tf_op jit(solution)/shard_map/ppermute | solution.py:207
  65.5 31.3 %shard_map.29 = bf16[256,4096]{1,0:T(8,128)(2,1)} custom-call(s32[2]{0:T(128)S(1)} %pad_add_fusion.meta_ref, bf16[32,2,32,1024]{3,2,1,0:T(8,128)(2,1)} %refs_0_.3, bf16[32,2,32,512]{3,2,1,0:T(8,128)(2,1)S(1)} %collective-permute-done.3.refs_1_, bf16[32,2,32,512]{3,2,1,0:T(8,128)(2,1)} %collective-permute-done.4.refs_2_, ...), custom_call_target="tpu_custom_call" | custom-call | flops 20000000000 | bytes 8388608 | tf_op jit(solution)/shard_map/pallas_call | solution.py:158
  96.7 0.0 copy-start
  96.7 0.0 reduce-scatter.2.cloned.1.call-update
  96.8 0.6 copy-done
  97.4 1.7 collective-permute-start.1
  99.1 0.0 collective-permute-start
  99.2 1.8 collective-permute-done.1
  100.9 0.0 collective-permute-start.2
  100.9 0.0 collective-permute-done
  100.9 1.1 collective-permute-done.2
  102.1 0.1 add_compare_fusion
  102.1 40.1 %reduce-scatter.2.cloned.1.call-done = bf16[64,4096]{1,0:T(8,128)(2,1)} async-done(((bf16[256,4096]{1,0:T(8,128)(2,1)}), bf16[64,4096]{1,0:T(8,128)(2,1)}) %reduce-scatter.2.cloned.1.call-update) | async-done | bytes 524304 | tf_op jit(solution)/shard_map/reduce_scatter | solution.py:209
  142.3 1.1 copy.15
  143.4 0.3 fusion.3
  143.8 0.2 pad_maximum_fusion.1
  144.0 1.5 collective-permute-start.7
  145.4 0.1 and_and_fusion
  145.5 1.0 copy.10
  146.6 2.5 %convert_element_type.20 = f32[64,32,128]{1,2,0:T(8,128)} convert(bf16[64,32,128]{1,2,0:T(8,128)(2,1)S(1)} %copy.10) | non-fusion elementwise | flops 262144 | bytes 1572864 | tf_op jit(solution)/shard_map/convert_element_type | solution.py:213
  149.1 1.1 slice.26
  150.2 0.2 pad_maximum_fusion.2
  150.3 1.3 collective-permute-start.8
  151.6 1.6 copy.11
  153.2 0.0 collective-permute-done.7
  153.2 0.2 fusion.5
  153.4 4.6 %collective-permute-done.8 = bf16[16,32,128]{2,1,0:T(8,128)(2,1)S(1)} collective-permute-done((bf16[16,32,128]{2,1,0:T(8,128)(2,1)S(1)}, bf16[16,32,128]{2,1,0:T(8,128)(2,1)S(1)}, u32[]{:S(2)}, u32[]{:S(2)}) %collective-permute-start.8) | collective-permute-done | bytes 131104 | tf_op jit(solution)/shard_map/ppermute | solution.py:211
  158.0 0.2 fusion.4
  158.2 3.6 %slice_select_fusion = (f32[64,32,32]{1,2,0:T(8,128)}, f32[64,32,32]{1,2,0:T(8,128)S(1)}, f32[64,32,32]{1,2,0:T(8,128)}) fusion(f32[64,32,128]{1,2,0:T(8,128)} %convert_element_type.20, pred[]{:T(512)S(6)} %eq.8, bf16[16,32,32]{2,1,0:T(8,128)(2,1)S(1)} %get-tuple-element.27, bf16[16,32,32]{2,1,0:T(8,128)(2,1)S(1)} %get-tuple-element.28, ...), kind=kLoop, calls=%fused_computation.10 | loop fusion | flops 720896 | bytes 1835009 | tf_op jit(solution)/shard_map/jit(_where)/select_n | solution.py:216
  161.8 0.3 copy.14
  162.2 1.6 copy.13
  163.7 2.5 %copy.12 = f32[64,32,32]{2,1,0:T(8,128)} copy(f32[64,32,32]{1,2,0:T(8,128)} %get-tuple-element.9) | data formatting | bytes 524288 | tf_op jit(solution)/shard_map/jit(_where)/select_n | solution.py:216
  166.3 3.1 %maximum_select_fusion = f32[64,32,128]{2,1,0:T(8,128)} fusion(f32[64,32,32]{2,1,0:T(8,128)S(1)} %copy.14, f32[64,32,32]{2,1,0:T(8,128)S(1)} %copy.13, f32[64,32,32]{2,1,0:T(8,128)} %copy.12, f32[64,32,32]{2,1,0:T(8,128)S(1)} %copy.11, pred[32,128]{1,0:T(8,128)(4,1)S(1)} %and_and_fusion), kind=kLoop, calls=%fused_computation.12 | loop fusion | flops 1048576 | bytes 2101248 | tf_op jit(solution)/shard_map/jit(_where)/select_n | solution.py:227
  (7 shorter events, 0.0 us)
Async XLA Ops:
  6.5 135.7 %reduce-scatter.2.cloned.1.call-start = ((), (), s32[]{:S(2)}) async-start(), calls=%async_computation.1 | async-start | bytes 2621440 | tf_op jit(solution)/shard_map/reduce_scatter | solution.py:209
  11.4 7.9 %collective-permute-start.5 = (bf16[32,2,32,512]{3,2,1,0:T(8,128)(2,1)}, bf16[32,2,32,512]{3,2,1,0:T(8,128)(2,1)}, u32[]{:S(2)}, u32[]{:S(2)}) collective-permute-start(bf16[32,2,32,512]{3,2,1,0:T(8,128)(2,1)} %get-tuple-element.12), channel_id=1, source_target_pairs={{0,4},{4,0},{8,12},{12,8},{1,5},{5,1},{9,13},{13,9},{2,6},{6,2},{1... | collective-permute-start | bytes 6291464 | tf_op jit(solution)/shard_map/ppermute | solution.py:188
  11.9 49.1 %collective-permute-start.4 = (bf16[32,2,32,512]{3,2,1,0:T(8,128)(2,1)}, bf16[32,2,32,512]{3,2,1,0:T(8,128)(2,1)}, u32[]{:S(2)}, u32[]{:S(2)}) collective-permute-start(bf16[32,2,32,512]{3,2,1,0:T(8,128)(2,1)} %get-tuple-element.12), channel_id=1, source_target_pairs={{0,8},{4,12},{8,0},{12,4},{1,9},{5,13},{9,1},{13,5},{2,10},{6,14},... | collective-permute-start | bytes 6291464 | tf_op jit(solution)/shard_map/ppermute | solution.py:187
  14.4 46.7 %collective-permute-start.3 = (bf16[32,2,32,512]{3,2,1,0:T(8,128)(2,1)}, bf16[32,2,32,512]{3,2,1,0:T(8,128)(2,1)S(1)}, u32[]{:S(2)}, u32[]{:S(2)}) collective-permute-start(bf16[32,2,32,512]{3,2,1,0:T(8,128)(2,1)} %get-tuple-element.13), channel_id=1, source_target_pairs={{0,4},{4,0},{8,12},{12,8},{1,5},{5,1},{9,13},{13,9},{2,6},{6,2},{1... | collective-permute-start | bytes 6291464 | tf_op jit(solution)/shard_map/ppermute | solution.py:189
  61.0 4.5 %collective-permute-start.6 = (bf16[32,2,32,512]{3,2,1,0:T(8,128)(2,1)}, bf16[32,2,32,512]{3,2,1,0:T(8,128)(2,1)}, u32[]{:S(2)}, u32[]{:S(2)}) collective-permute-start(bf16[32,2,32,512]{3,2,1,0:T(8,128)(2,1)} %collective-permute-done.4.refs_2_), channel_id=1, source_target_pairs={{0,4},{4,0},{8,12},{12,8},{1,5},{5,1},{9,13},{13,9},{2,6},{6,2},{1... | collective-permute-start | bytes 6291464 | tf_op jit(solution)/shard_map/ppermute | solution.py:207
  96.7 0.7 copy-start
  97.4 3.5 %collective-permute-start.1 = (s32[32]{0:T(128)S(1)}, s32[32]{0:T(128)S(1)}, u32[]{:S(2)}, u32[]{:S(2)}) collective-permute-start(s32[32]{0:T(128)S(1)} %copy-done), channel_id=1, source_target_pairs={{0,8},{4,12},{8,0},{12,4},{1,9},{5,13},{9,1},{13,5},{2,10},{6,14},... | collective-permute-start | bytes 392 | tf_op jit(solution)/shard_map/ppermute | solution.py:191
  99.1 1.8 %collective-permute-start = (s32[32]{0:T(128)S(1)}, s32[32]{0:T(128)S(1)}, u32[]{:S(2)}, u32[]{:S(2)}) collective-permute-start(s32[32]{0:T(128)S(1)} %copy-done), channel_id=1, source_target_pairs={{0,4},{4,0},{8,12},{12,8},{1,5},{5,1},{9,13},{13,9},{2,6},{6,2},{1... | collective-permute-start | bytes 392 | tf_op jit(solution)/shard_map/ppermute | solution.py:190
  100.9 1.1 collective-permute-start.2
  144.0 9.2 %collective-permute-start.7 = (bf16[16,32,128]{2,1,0:T(8,128)(2,1)S(1)}, bf16[16,32,128]{2,1,0:T(8,128)(2,1)S(1)}, u32[]{:S(2)}, u32[]{:S(2)}) collective-permute-start(bf16[16,32,128]{2,1,0:T(8,128)(2,1)S(1)} %pad_maximum_fusion.1), channel_id=1, source_target_pairs={{8,4},{12,0},{9,5},{13,1},{10,6},{14,2},{11,7},{15,3},{24,20},{28,... | collective-permute-start | bytes 393224 | tf_op jit(solution)/shard_map/ppermute | solution.py:212
  150.3 7.7 %collective-permute-start.8 = (bf16[16,32,128]{2,1,0:T(8,128)(2,1)S(1)}, bf16[16,32,128]{2,1,0:T(8,128)(2,1)S(1)}, u32[]{:S(2)}, u32[]{:S(2)}) collective-permute-start(bf16[16,32,128]{2,1,0:T(8,128)(2,1)S(1)} %pad_maximum_fusion.2), channel_id=1, source_target_pairs={{8,0},{12,4},{9,1},{13,5},{10,2},{14,6},{11,3},{15,7},{24,16},{28,... | collective-permute-start | bytes 393224 | tf_op jit(solution)/shard_map/ppermute | solution.py:211
Sparse Core Ops, SparseCore 0:
  96.9 45.3 reduce-scatter.1

commit v5 on v4

--- a/solution.py
+++ b/solution.py
@@ -72,9 +72,13 @@
     ).astype(jnp.float32)
 
 
-def correlate_kernel(crossing, starting, meta_ref, *refs):
+def correlate_kernel(crossing, starting, last, meta_ref, *refs):
     if crossing:
-        own, near, far_a, far_b, table, before, out, acc, spread, gram = refs
+        if last:
+            own, near, far_a, far_b, table, before, out, acc, spread, gram = refs
+        else:
+            own, near, far_a, far_b, table, before, out, spread, gram = refs
+            acc = out
         sources = (own, near, far_a, far_b)
     else:
         if starting:
@@ -131,24 +135,26 @@
 
     lax.fori_loop(0, 16, two_rows, 0, unroll=16)
 
-    if crossing:
+    if last:
         @pl.when(step == pl.num_programs(0) - 1)
         def _():
             out[...] = (acc[...] * (1.0 / math.sqrt(S * F))).astype(out.dtype)
 
 
-def correlate(meta, own, near, far, table, before, skip, chunks):
+def correlate(meta, own, near, far, table, before, skip, chunks, last):
     crossing = far is not None
     block = (S, 2, 32, BINS)
     placed = pl.BlockSpec(block, lambda k, m: (0, 0, 0, m[0] + skip + k))
     near_by = pl.BlockSpec(block, lambda k, m: (0, 0, 0, skip + k))
+    far_by = pl.BlockSpec(block, lambda k, m: (0, 0, 0, k))
     table_spec = pl.BlockSpec((1, L, 2 * BINS), lambda k, m: (m[0] + skip + k, 0, 0))
     whole = pl.BlockSpec((L, 4096), lambda k, m: (0, 0))
     scratch = [pltpu.VMEM((2 * S * BINS, 128), jnp.float32), pltpu.VMEM((2 * BINS * 32, 128), jnp.float32)]
     if crossing:
-        in_specs = [placed, near_by, near_by, near_by, table_spec, whole]
+        in_specs = [placed, near_by, far_by, far_by, table_spec, whole]
         operands = (own, near, far[0], far[1], table, before)
-        scratch = [pltpu.VMEM((L, 4096), jnp.float32)] + scratch
+        if last:
+            scratch = [pltpu.VMEM((L, 4096), jnp.float32)] + scratch
     else:
         in_specs = [placed, near_by, table_spec]
         operands = (own, near, table)
@@ -156,8 +162,8 @@
             in_specs.append(whole)
             operands += (before,)
     return pl.pallas_call(
-        functools.partial(correlate_kernel, crossing, before is None),
-        out_shape=jax.ShapeDtypeStruct((L, 4096), jnp.bfloat16 if crossing else jnp.float32),
+        functools.partial(correlate_kernel, crossing, before is None, last),
+        out_shape=jax.ShapeDtypeStruct((L, 4096), jnp.bfloat16 if last else jnp.float32),
         grid_spec=pltpu.PrefetchScalarGridSpec(
             num_scalar_prefetch=1, grid=(chunks,), in_specs=in_specs, out_specs=whole, scratch_shapes=scratch
         ),
@@ -182,9 +188,14 @@
     x, core = wide_pos // 2, wide_pos % 2
     over_x = [(0, 2), (1, 3), (2, 0), (3, 1)]
     on_chip = [(0, 1), (1, 0), (2, 3), (3, 2)]
-    leaving = lax.dynamic_slice_in_dim(spectra, (1 - x) * half, half, 3)
-    staying = lax.dynamic_slice_in_dim(spectra, x * half, half, 3)
-    far_a = lax.ppermute(leaving, "wide", over_x)
+    quarter = half // 2
+    early = lax.dynamic_slice_in_dim(spectra, (1 - x) * half, quarter, 3)
+    far_a = lax.ppermute(early, "wide", over_x)
+    early, later = lax.optimization_barrier((early, spectra))
+    late = lax.dynamic_slice_in_dim(later, (1 - x) * half + quarter, quarter, 3)
+    late_a = lax.ppermute(late, "wide", over_x)
+    leaving = lax.dynamic_slice_in_dim(later, (1 - x) * half, half, 3)
+    staying = lax.dynamic_slice_in_dim(later, x * half, half, 3)
     near_first = lax.ppermute(leaving, "wide", on_chip)
     near_second = lax.ppermute(staying, "wide", on_chip)
     live_near = lax.ppermute(live, "wide", on_chip)
@@ -202,10 +213,16 @@
     chunks = half // BINS
     first = jnp.stack([(1 - x) * chunks, x]).astype(jnp.int32)
     second = jnp.stack([x * chunks, x]).astype(jnp.int32)
-    before = correlate(first, spectra, near_first, None, table, None, 0, chunks)
+    before = correlate(first, spectra, near_first, None, table, None, 0, chunks, False)
     far_a, before = lax.optimization_barrier((far_a, before))
     far_b = lax.ppermute(far_a, "wide", on_chip)
-    partial = correlate(second, spectra, near_second, (far_a, far_b), table, before, 0, chunks)
+    part = chunks // 2
+    before = correlate(second, spectra, near_second, (far_a, far_b), table, before, 0, part, False)
+    late_a, before = lax.optimization_barrier((late_a, before))
+    late_b = lax.ppermute(late_a, "wide", on_chip)
+    partial = correlate(
+        second, spectra, near_second, (late_a, late_b), table, before, part, chunks - part, True
+    )
     mine = lax.psum_scatter(partial, "narrow", scatter_dimension=0, tiled=True)
     mine = mine.reshape(-1, 32, 128)
     back_a = unfold(lax.ppermute(fold(mine[:, :, 64:96]), "wide", [(2, 0), (3, 1)]))

time: 177 us -> 180 us (1.017)
  waiting for transfers between devices: 63.5 us -> 55.4 us
  Pallas kernels: 61.5 us -> 67.1 us
  local copies, waits for them, and re-layouts: 15.4 us -> 19.3 us
  starting transfers between devices: 7.68 us -> 9.48 us
    pallas_call x2 -> x3, Pallas kernels: 61.5 us -> 67.1 us  [correlate(): pl.pallas_call(functools.partial(correlate_kernel, crossing, before is No...]
    ppermute x1, waiting for transfers between devices: 0.01 us -> 5.34 us  [two_chips(): lax.ppermute(fold(mine[:, :, 96:]), 'wide', [(2, 1), (3, 0)])]
    ppermute x1, waiting for transfers between devices: 4.64 us -> 0.01 us  [two_chips(): lax.ppermute(fold(mine[:, :, 64:96]), 'wide', [(2, 0), (3, 1)])]
    dynamic_slice x1 -> x3, local copies, waits for them, and re-layouts: 4.89 us -> 9.39 us  [the longest x1 4.79 us: two_chips(): leaving = lax.dynamic_slice_in_dim(later, (1 - x) * half, half, 3)]
    ppermute x1, waiting for transfers between devices: 4.42 us -> 0.01 us  [two_chips(): far_b = lax.ppermute(far_a, 'wide', on_chip)]
    ppermute x1 -> x3, waiting for transfers between devices: 11.4 us -> 8.22 us  [the longest x1 5.35 us: two_chips(): late_a = lax.ppermute(late, 'wide', over_x)]
    add x1, local copies, waits for them, and re-layouts: 0.33 us -> 2.55 us  [two_chips(): far_2 = mine[:, :, 96:] + jnp.swapaxes(back_b, 1, 2).astype(jnp.float32)]
    select_n x1, local copies, waits for them, and re-layouts: 2.54 us -> 0.33 us  [two_chips(): q1 = jnp.where(core == 0, mine[:, :, 32:64], far_2)]
  transfers between devices with their start and end apart: 10 -> 12, of which waited for: 6 -> 6; matrix products, arithmetic and copies ran while one was open for 7% -> 6% of each run, Pallas kernels for 17% -> 27%
where the time goes in v5:
time: 180 us
  Pallas kernels  67.1 us (37%)
  waiting for transfers between devices  55.4 us (31%)
  local copies, waits for them, and re-layouts  19.3 us (11%)
  other arithmetic  15.2 us (8%)
  between operations  13.6 us (8%)
  starting transfers between devices  9.48 us (5%)
    pallas_call x3, Pallas kernels, correlate(): pl.pallas_call(functools.partial(correlate_kernel, crossing, before is No...  67.1 us
    reduce_scatter x1, waiting for transfers between devices, two_chips(): mine = lax.psum_scatter(partial, 'narrow', scatter_dimension=0, tiled=True)  38.9 us
    ppermute x1, waiting for transfers between devices, two_chips(): late_a = lax.ppermute(late, 'wide', over_x)  5.35 us
    ppermute x1, waiting for transfers between devices, two_chips(): lax.ppermute(fold(mine[:, :, 96:]), 'wide', [(2, 1), (3, 0)])  5.34 us
    dynamic_slice x1, local copies, waits for them, and re-layouts, two_chips(): leaving = lax.dynamic_slice_in_dim(later, (1 - x) * half, half, 3)  4.79 us
    another operation x1, other arithmetic  4.52 us
    select_n x1, other arithmetic, two_chips(): q1 = jnp.where(core == 0, mine[:, :, 32:64], far_2)  3.62 us
  transfers between devices with their start and end apart: 12, of which 6 were waited for; matrix products, arithmetic and copies ran while one was open for 6% of the time, Pallas kernels for 27%

profile of v5, /device:TPU:0, one launch (start us, length us, event | category | flops | bytes accessed | tf_op | source)
XLA Modules:
  0.0 180.0 jit_solution(10169804804813900817)
XLA Ops:
  6.5 2.3 %constant_dynamic-slice_fusion.3 = bf16[32,2,32,256]{3,2,1,0:T(8,128)(2,1)} fusion(bf16[32,2,32,1024]{3,2,1,0:T(8,128)(2,1)} %refs_0_.5, s32[]{:T(128)S(6)} %select_n.51), kind=kLoop, calls=%fused_computation.23 | loop fusion | bytes 2097156 | tf_op jit(solution)/shard_map/dynamic_slice | solution.py:192
  8.8 4.8 %constant_dynamic-slice_fusion = (bf16[32,2,32,512]{3,2,1,0:T(8,128)(2,1)}, bf16[32,2,32,512]{3,2,1,0:T(8,128)(2,1)}) fusion(bf16[32,2,32,1024]{3,2,1,0:T(8,128)(2,1)} %refs_0_.5, s32[]{:T(128)S(6)} %select_n.51, s32[]{:T(128)S(6)} %select_n.52), kind=kLoop, calls=%fused_computation.20 | loop fusion | bytes 8388616 | tf_op jit(solution)/shard_map/dynamic_slice | solution.py:197
  13.6 0.5 collective-permute-start.6
  14.1 2.5 %collective-permute-start.5 = (bf16[32,2,32,256]{3,2,1,0:T(8,128)(2,1)}, bf16[32,2,32,256]{3,2,1,0:T(8,128)(2,1)}, u32[]{:S(2)}, u32[]{:S(2)}) collective-permute-start(bf16[32,2,32,256]{3,2,1,0:T(8,128)(2,1)} %constant_dynamic-slice_fusion.3), channel_id=1, source_target_pairs={{0,8},{4,12},{8,0},{12,4},{1,9},{5,13},{9,1},{13,5},{2,10},{6,14},... | collective-permute-start | bytes 3145736 | tf_op jit(solution)/shard_map/ppermute | solution.py:193
  16.6 0.2 collective-permute-start.3
  16.8 0.1 pad_add_fusion.1.meta_ref
  16.9 4.5 %cosine_convert_fusion = (bf16[8,256,128]{2,1,0:T(8,128)(2,1)S(1)}, bf16[8,256,128]{2,1,0:T(8,128)(2,1)S(1)}) fusion(s32[256]{0:T(256)S(1)} %iota_add_fusion, s32[8,128]{1,0:T(8,128)S(1)} %add_add_fusion), kind=kLoop, calls=%fused_computation.14 | loop fusion | flops 4456448 | bytes 1053696 | tf_op jit(solution)/shard_map/convert.2
  21.4 0.1 pad_maximum_fusion.refs_2_.refs_4_
  21.6 30.2 %shard_map.28.refs_5_ = f32[256,4096]{1,0:T(8,128)} custom-call(s32[2]{0:T(128)S(1)} %pad_add_fusion.1.meta_ref, bf16[32,2,32,1024]{3,2,1,0:T(8,128)(2,1)} %refs_0_.5, bf16[32,2,32,512]{3,2,1,0:T(8,128)(2,1)} %collective-permute-done.6.refs_1_, bf16[8,256,256]{2,1,0:T(8,128)(2,1)S(1)} %pad_maximum_fusion.refs_2_.refs_4_), custom_call_target="tpu_custom_call" | custom-call | flops 20000000000 | bytes 8388608 | tf_op jit(solution)/shard_map/pallas_call | solution.py:164
  51.8 0.3 collective-permute-start.7
  52.1 2.3 %constant_dynamic-slice_fusion.1 = bf16[32,2,32,256]{3,2,1,0:T(8,128)(2,1)} fusion(bf16[32,2,32,1024]{3,2,1,0:T(8,128)(2,1)} %refs_0_.5, s32[]{:T(128)S(6)} %select_n.53), kind=kLoop, calls=%fused_computation.21 | loop fusion | bytes 2097156 | tf_op jit(solution)/shard_map/dynamic_slice | solution.py:195
  54.4 1.7 collective-permute-start.4
  56.1 0.1 pad_add_fusion.meta_ref
  56.2 0.0 collective-permute-done.3.refs_1_
  56.2 0.0 collective-permute-done.7.refs_3_
  56.2 18.6 %shard_map.29.refs_5_ = f32[256,4096]{1,0:T(8,128)} custom-call(s32[2]{0:T(128)S(1)} %pad_add_fusion.meta_ref, bf16[32,2,32,1024]{3,2,1,0:T(8,128)(2,1)} %refs_0_.5, bf16[32,2,32,512]{3,2,1,0:T(8,128)(2,1)S(1)} %collective-permute-done.3.refs_1_, bf16[32,2,32,256]{3,2,1,0:T(8,128)(2,1)} %collective-permute-done.5.refs_2_, ...), custom_call_target="tpu_custom_call" | custom-call | flops 10000000000 | bytes 8388608 | tf_op jit(solution)/shard_map/pallas_call | solution.py:164
  74.7 5.4 %collective-permute-done.4.refs_2_ = bf16[32,2,32,256]{3,2,1,0:T(8,128)(2,1)} collective-permute-done((bf16[32,2,32,256]{3,2,1,0:T(8,128)(2,1)}, bf16[32,2,32,256]{3,2,1,0:T(8,128)(2,1)}, u32[]{:S(2)}, u32[]{:S(2)}) %collective-permute-start.4) | collective-permute-done | bytes 1048608 | tf_op jit(solution)/shard_map/ppermute | solution.py:196
  80.1 2.9 %collective-permute-done.8.refs_3_ = bf16[32,2,32,256]{3,2,1,0:T(8,128)(2,1)S(1)} collective-permute-done((bf16[32,2,32,256]{3,2,1,0:T(8,128)(2,1)}, bf16[32,2,32,256]{3,2,1,0:T(8,128)(2,1)S(1)}, u32[]{:S(2)}, u32[]{:S(2)}) %collective-permute-start.8) | collective-permute-done | bytes 1048608 | tf_op jit(solution)/shard_map/ppermute | solution.py:222
  83.0 18.3 %shard_map.30 = bf16[256,4096]{1,0:T(8,128)(2,1)} custom-call(s32[2]{0:T(128)S(1)} %pad_add_fusion.meta_ref, bf16[32,2,32,1024]{3,2,1,0:T(8,128)(2,1)} %refs_0_.5, bf16[32,2,32,512]{3,2,1,0:T(8,128)(2,1)} %copy-done, bf16[32,2,32,256]{3,2,1,0:T(8,128)(2,1)} %collective-permute-done.4.refs_2_, bf16[32,2,32,256]{3,2,1,0:T(8,128)(2,1)S(1)} %collective-permute-done.8.refs_3_, ...), custom_call_target="tpu_custom_call" | custom-call | flops 10000000000 | bytes 8388608 | tf_op jit(solution)/shard_map/pallas_call | solution.py:164
  101.3 0.0 reduce-scatter.2.cloned.1.call-update
  101.3 0.6 copy-done.3
  101.9 1.7 collective-permute-start.1
  103.7 0.0 collective-permute-start
  103.7 1.7 collective-permute-done.1
  105.5 1.1 collective-permute-done.2
  106.6 0.1 add_compare_fusion
  106.7 38.9 %reduce-scatter.2.cloned.1.call-done = bf16[64,4096]{1,0:T(8,128)(2,1)} async-done(((bf16[256,4096]{1,0:T(8,128)(2,1)}), bf16[64,4096]{1,0:T(8,128)(2,1)}) %reduce-scatter.2.cloned.1.call-update) | async-done | bytes 524304 | tf_op jit(solution)/shard_map/reduce_scatter | solution.py:226
  145.6 1.1 copy.15
  146.8 1.0 fusion.3
  147.8 0.8 pad_maximum_fusion.2
  148.6 1.3 collective-permute-start.10
  149.9 0.1 and_and_fusion
  150.0 1.0 copy.10
  151.0 2.5 %convert_element_type.20 = f32[64,32,128]{1,2,0:T(8,128)} convert(bf16[64,32,128]{1,2,0:T(8,128)(2,1)S(1)} %copy.10) | non-fusion elementwise | flops 262144 | bytes 1572864 | tf_op jit(solution)/shard_map/convert_element_type | solution.py:230
  153.5 0.1 slice.26
  153.6 0.8 copy-done.1
  154.4 0.1 copy-done.2
  154.5 0.2 pad_maximum_fusion.1
  154.7 1.3 collective-permute-start.9
  156.0 0.3 copy.11
  156.3 0.2 fusion.4
  156.5 5.3 %collective-permute-done.9 = bf16[16,32,128]{2,1,0:T(8,128)(2,1)S(1)} collective-permute-done((bf16[16,32,128]{2,1,0:T(8,128)(2,1)S(1)}, bf16[16,32,128]{2,1,0:T(8,128)(2,1)S(1)}, u32[]{:S(2)}, u32[]{:S(2)}) %collective-permute-start.9) | collective-permute-done | bytes 131104 | tf_op jit(solution)/shard_map/ppermute | solution.py:229
  161.8 0.2 fusion.5
  162.0 3.6 %slice_select_fusion = (f32[64,32,32]{1,2,0:T(8,128)S(1)}, f32[64,32,32]{1,2,0:T(8,128)}, f32[64,32,32]{1,2,0:T(8,128)}) fusion(f32[64,32,128]{1,2,0:T(8,128)} %convert_element_type.20, pred[]{:T(512)S(6)} %eq.8, bf16[16,32,32]{2,1,0:T(8,128)(2,1)S(1)} %get-tuple-element.33, bf16[16,32,32]{2,1,0:T(8,128)(2,1)S(1)} %get-tuple-element.34, ...), kind=kLoop, calls=%fused_computation.10 | loop fusion | flops 720896 | bytes 1835009 | tf_op jit(solution)/shard_map/jit(_where)/select_n | solution.py:233
  165.6 0.3 copy.12
  166.0 1.6 copy.13
  167.5 2.5 %copy.14 = f32[64,32,32]{2,1,0:T(8,128)} copy(f32[64,32,32]{1,2,0:T(8,128)} %get-tuple-element.16) | data formatting | bytes 524288 | tf_op jit(solution)/shard_map/add | solution.py:232
  170.1 3.1 %maximum_select_fusion = f32[64,32,128]{2,1,0:T(8,128)} fusion(f32[64,32,32]{2,1,0:T(8,128)} %copy.14, f32[64,32,32]{2,1,0:T(8,128)S(1)} %copy.13, f32[64,32,32]{2,1,0:T(8,128)S(1)} %copy.12, f32[64,32,32]{2,1,0:T(8,128)S(1)} %copy.11, pred[32,128]{1,0:T(8,128)(4,1)S(1)} %and_and_fusion), kind=kLoop, calls=%fused_computation.12 | loop fusion | flops 1048576 | bytes 2101248 | tf_op jit(solution)/shard_map/jit(_where)/select_n | solution.py:244
  (19 shorter events, 0.1 us)
Async XLA Ops:
  6.5 139.1 %reduce-scatter.2.cloned.1.call-start = ((), (), s32[]{:S(2)}) async-start(), calls=%async_computation.1 | async-start | bytes 2621440 | tf_op jit(solution)/shard_map/reduce_scatter | solution.py:226
  13.6 7.9 %collective-permute-start.6 = (bf16[32,2,32,512]{3,2,1,0:T(8,128)(2,1)}, bf16[32,2,32,512]{3,2,1,0:T(8,128)(2,1)}, u32[]{:S(2)}, u32[]{:S(2)}) collective-permute-start(bf16[32,2,32,512]{3,2,1,0:T(8,128)(2,1)} %get-tuple-element.18), channel_id=1, source_target_pairs={{0,4},{4,0},{8,12},{12,8},{1,5},{5,1},{9,13},{13,9},{2,6},{6,2},{1... | collective-permute-start | bytes 6291464 | tf_op jit(solution)/shard_map/ppermute | solution.py:199
  14.1 37.7 %collective-permute-start.5 = (bf16[32,2,32,256]{3,2,1,0:T(8,128)(2,1)}, bf16[32,2,32,256]{3,2,1,0:T(8,128)(2,1)}, u32[]{:S(2)}, u32[]{:S(2)}) collective-permute-start(bf16[32,2,32,256]{3,2,1,0:T(8,128)(2,1)} %constant_dynamic-slice_fusion.3), channel_id=1, source_target_pairs={{0,8},{4,12},{8,0},{12,4},{1,9},{5,13},{9,1},{13,5},{2,10},{6,14},... | collective-permute-start | bytes 3145736 | tf_op jit(solution)/shard_map/ppermute | solution.py:193
  16.6 39.6 %collective-permute-start.3 = (bf16[32,2,32,512]{3,2,1,0:T(8,128)(2,1)}, bf16[32,2,32,512]{3,2,1,0:T(8,128)(2,1)S(1)}, u32[]{:S(2)}, u32[]{:S(2)}) collective-permute-start(bf16[32,2,32,512]{3,2,1,0:T(8,128)(2,1)} %get-tuple-element.19), channel_id=1, source_target_pairs={{0,4},{4,0},{8,12},{12,8},{1,5},{5,1},{9,13},{13,9},{2,6},{6,2},{1... | collective-permute-start | bytes 6291464 | tf_op jit(solution)/shard_map/ppermute | solution.py:200
  51.8 4.4 %collective-permute-start.7 = (bf16[32,2,32,256]{3,2,1,0:T(8,128)(2,1)}, bf16[32,2,32,256]{3,2,1,0:T(8,128)(2,1)}, u32[]{:S(2)}, u32[]{:S(2)}) collective-permute-start(bf16[32,2,32,256]{3,2,1,0:T(8,128)(2,1)} %collective-permute-done.5.refs_2_), channel_id=1, source_target_pairs={{0,4},{4,0},{8,12},{12,8},{1,5},{5,1},{9,13},{13,9},{2,6},{6,2},{1... | collective-permute-start | bytes 3145736 | tf_op jit(solution)/shard_map/ppermute | solution.py:218
  54.4 25.7 %collective-permute-start.4 = (bf16[32,2,32,256]{3,2,1,0:T(8,128)(2,1)}, bf16[32,2,32,256]{3,2,1,0:T(8,128)(2,1)}, u32[]{:S(2)}, u32[]{:S(2)}) collective-permute-start(bf16[32,2,32,256]{3,2,1,0:T(8,128)(2,1)} %constant_dynamic-slice_fusion.1), channel_id=1, source_target_pairs={{0,8},{4,12},{8,0},{12,4},{1,9},{5,13},{9,1},{13,5},{2,10},{6,14},... | collective-permute-start | bytes 3145736 | tf_op jit(solution)/shard_map/ppermute | solution.py:196
  56.2 18.6 %copy-start = (bf16[32,2,32,512]{3,2,1,0:T(8,128)(2,1)}, bf16[32,2,32,512]{3,2,1,0:T(8,128)(2,1)S(1)}, u32[]{:S(2)}) copy-start(bf16[32,2,32,512]{3,2,1,0:T(8,128)(2,1)S(1)} %collective-permute-done.3.refs_1_) | copy-start | bytes 6291460
  80.1 2.9 %collective-permute-start.8 = (bf16[32,2,32,256]{3,2,1,0:T(8,128)(2,1)}, bf16[32,2,32,256]{3,2,1,0:T(8,128)(2,1)S(1)}, u32[]{:S(2)}, u32[]{:S(2)}) collective-permute-start(bf16[32,2,32,256]{3,2,1,0:T(8,128)(2,1)} %collective-permute-done.4.refs_2_), channel_id=1, source_target_pairs={{0,4},{4,0},{8,12},{12,8},{1,5},{5,1},{9,13},{13,9},{2,6},{6,2},{1... | collective-permute-start | bytes 3145736 | tf_op jit(solution)/shard_map/ppermute | solution.py:222
  101.3 0.7 copy-start.3
  101.9 3.5 %collective-permute-start.1 = (s32[32]{0:T(128)S(1)}, s32[32]{0:T(128)S(1)}, u32[]{:S(2)}, u32[]{:S(2)}) collective-permute-start(s32[32]{0:T(128)S(1)} %copy-done.3), channel_id=1, source_target_pairs={{0,8},{4,12},{8,0},{12,4},{1,9},{5,13},{9,1},{13,5},{2,10},{6,14},... | collective-permute-start | bytes 392 | tf_op jit(solution)/shard_map/ppermute | solution.py:202
  103.7 1.8 %collective-permute-start = (s32[32]{0:T(128)S(1)}, s32[32]{0:T(128)S(1)}, u32[]{:S(2)}, u32[]{:S(2)}) collective-permute-start(s32[32]{0:T(128)S(1)} %copy-done.3), channel_id=1, source_target_pairs={{0,4},{4,0},{8,12},{12,8},{1,5},{5,1},{9,13},{13,9},{2,6},{6,2},{1... | collective-permute-start | bytes 392 | tf_op jit(solution)/shard_map/ppermute | solution.py:201
  105.5 1.1 collective-permute-start.2
  148.6 7.7 %collective-permute-start.10 = (bf16[16,32,128]{2,1,0:T(8,128)(2,1)}, bf16[16,32,128]{2,1,0:T(8,128)(2,1)S(1)}, u32[]{:S(2)}, u32[]{:S(2)}) collective-permute-start(bf16[16,32,128]{2,1,0:T(8,128)(2,1)} %pad_maximum_fusion.2), channel_id=1, source_target_pairs={{8,0},{12,4},{9,1},{13,5},{10,2},{14,6},{11,3},{15,7},{24,16},{28,... | collective-permute-start | bytes 393224 | tf_op jit(solution)/shard_map/ppermute | solution.py:228
  153.5 0.9 copy-start.1
  153.5 1.0 copy-start.2
  154.7 7.2 %collective-permute-start.9 = (bf16[16,32,128]{2,1,0:T(8,128)(2,1)S(1)}, bf16[16,32,128]{2,1,0:T(8,128)(2,1)S(1)}, u32[]{:S(2)}, u32[]{:S(2)}) collective-permute-start(bf16[16,32,128]{2,1,0:T(8,128)(2,1)S(1)} %pad_maximum_fusion.1), channel_id=1, source_target_pairs={{8,4},{12,0},{9,5},{13,1},{10,6},{14,2},{11,7},{15,3},{24,20},{28,... | collective-permute-start | bytes 393224 | tf_op jit(solution)/shard_map/ppermute | solution.py:229
Sparse Core Ops, SparseCore 0:
  101.4 44.1 reduce-scatter.1
